TPU v7x, 128 devices: a whole 4x4x4 slice. The times are simulated.
128 devices in a mesh: req: 32 (over z, y, core), head: 4 (over x).
Axes of the slice: x: 4, y: 4, z: 4, core: 2. Of those that a mesh axis runs over, the one named last changes fastest.
Arguments:
- queries: bfloat16 [98304, 8, 128], P('req', 'head'), may hold values from -6 to 6
- key_rows: bfloat16 [98304, 8, 128], P('req', 'head'), may hold values from -6 to 6
- values: bfloat16 [98304, 16, 128], P('req', 'head'), may hold values from -6 to 6
- gate_input: bfloat16 [98304, 16, 128], P('req', 'head'), may hold values from -6 to 6
- write_rate: float32 [98304, 16], P('req', 'head'), may hold values from 0.1 to 0.9
- log_decay: float32 [98304, 16], P('req', 'head'), may hold values from -1 to 0
- norm_gain: float32 [128], replicated, may hold values from 0.1 to 1.9
- out_weight: bfloat16 [2048, 2048], P('head'), may hold values from -0.125 to 0.125
- cache_states: float32 [256, 16, 128, 128], P('req', 'head'), may hold values from -6 to 6
- cache_owner: int32 [768], replicated, may hold values from 0 to 31, as said below
- cache_slot: int32 [768], replicated, may hold values from 0 to 7
- suffix_blocks: int32 [768], replicated, may hold values from 1 to 2, as said below
- new_slot: int32 [768], replicated, may hold values from 0 to 23, as said below
Outputs:
- layer_out: bfloat16 [98304, 2048], P(('req', 'head'))
- new_cache: float32 [768, 16, 128, 128], P('req', 'head')
Inputs may be any that keep to these rules, and one draw needn't show every extreme that they name: `cache_owner`: the 24 requests of one device name one owner at most 1 times, and some owner that many times; for every position within a device's requests, each owner is named by exactly one device, so each owner is named by exactly 24 requests. `suffix_blocks`: the largest, 2, is reached. `new_slot`: the 24 requests that name one owner take its 24 new slots one each.
All inputs are finite; a program needn't handle non-finite values.
Results may differ from a plain program's by a relative error of at most 0.019.
Values may be sent and summed in bfloat16 or wider, within the bound.
No kernel may reach another device: no remote copies, remote signals or barrier semaphores. Data moves between devices by JAX's collectives and lax.ppermute only.
A program may use at most 256 MiB of HBM per device.

v0:
```python
import jax
import jax.numpy as jnp
from jax import lax
from jax.sharding import PartitionSpec as P

BLOCK = 64
TAIL_POSITIONS = 128


HIGHEST = lax.Precision.HIGHEST
EPSILON = 1e-06


def unit_rows(vectors):
    vectors = vectors.astype(jnp.float32)
    return vectors * lax.rsqrt(jnp.sum(vectors * vectors, axis=-1, keepdims=True) + EPSILON)


def prepare(queries, key_rows, values, write_rate, log_decay):
    steps_in = log_decay.shape[-1]
    query_wide = queries.astype(jnp.float32)
    key_wide = key_rows.astype(jnp.float32)
    running = jnp.cumsum(log_decay, axis=-1)
    row_ids = lax.broadcasted_iota(jnp.int32, (steps_in, steps_in), 0)
    col_ids = lax.broadcasted_iota(jnp.int32, (steps_in, steps_in), 1)
    spacing = running[..., :, None] - running[..., None, :]
    strict = row_ids > col_ids
    within = row_ids >= col_ids
    fade_strict = jnp.where(strict, jnp.exp(jnp.where(strict, spacing, 0.0)), 0.0)
    fade_within = jnp.where(within, jnp.exp(jnp.where(within, spacing, 0.0)), 0.0)
    affinity = jnp.einsum(
        "...td,...sd->...ts", key_rows, key_rows, preferred_element_type=jnp.float32
    )
    system = write_rate[..., :, None] * affinity * fade_strict + jnp.eye(
        steps_in, dtype=jnp.float32
    )
    growth = jnp.exp(running)
    targets = jnp.concatenate(
        [
            write_rate[..., None] * values.astype(jnp.float32),
            (write_rate * growth)[..., None] * key_wide,
        ],
        axis=-1,
    )
    solved = lax.linalg.triangular_solve(
        system, targets, left_side=True, lower=True, unit_diagonal=True
    )
    value_width = values.shape[-1]
    corrected = solved[..., :value_width]
    projector = solved[..., value_width:]
    scores = (
        jnp.einsum("...td,...sd->...ts", queries, key_rows, preferred_element_type=jnp.float32)
        * fade_within
    )
    query_fade = query_wide * growth[..., None]
    ending = running[..., -1:]
    key_fade = key_wide * jnp.exp(ending - running)[..., None]
    return (query_fade, key_fade, corrected, projector, scores, jnp.exp(ending[..., 0]))


def advance(carried, query_fade, key_fade, corrected, projector, scores, retained):
    fresh_values = corrected - jnp.einsum(
        "...tk,...kv->...tv", projector, carried, precision=HIGHEST
    )
    block_out = jnp.einsum("...tk,...kv->...tv", query_fade, carried, precision=HIGHEST)
    block_out = block_out + jnp.einsum(
        "...ts,...sv->...tv", scores, fresh_values, precision=HIGHEST
    )
    updated = retained[..., None, None] * carried + jnp.einsum(
        "...tk,...tv->...kv", key_fade, fresh_values, precision=HIGHEST
    )
    return (block_out, updated)


def arrange(source, requests):
    blocks_per = source.shape[0] // requests // BLOCK
    shaped = source.reshape((requests, blocks_per, BLOCK) + source.shape[1:])
    if shaped.ndim == 5:
        return jnp.transpose(shaped, (0, 3, 1, 2, 4))
    return jnp.transpose(shaped, (0, 3, 1, 2))


def local(
    queries,
    key_rows,
    values,
    gate_input,
    write_rate,
    log_decay,
    norm_gain,
    out_weight,
    cache_states,
    cache_owner,
    cache_slot,
    suffix_blocks,
    new_slot,
):
    owner_count = lax.axis_size("req")
    device = lax.axis_index("req")
    requests = queries.shape[0] // TAIL_POSITIONS
    repeats = values.shape[1] // queries.shape[1]
    pair_cap = -(-requests // owner_count)
    key_width = queries.shape[2]
    pair_ids = jnp.arange(pair_cap, dtype=jnp.int32)
    request_ids = jnp.arange(requests, dtype=jnp.int32)
    my_owner = lax.dynamic_slice_in_dim(cache_owner, device * requests, requests)
    my_blocks = lax.dynamic_slice_in_dim(suffix_blocks, device * requests, requests)
    same_owner = my_owner[:, None] == my_owner[None, :]
    my_rank = jnp.sum(
        (same_owner & (request_ids[None, :] < request_ids[:, None])).astype(jnp.int32), axis=1
    )
    naming = cache_owner.reshape(owner_count, requests) == device
    rank_rows = jnp.cumsum(naming.astype(jnp.int32), axis=1) - 1
    matched = naming[:, None, :] & (rank_rows[:, None, :] == pair_ids[None, :, None])
    present = jnp.any(matched, axis=2)
    which_req = jnp.sum(jnp.where(matched, request_ids, 0), axis=2)
    wanted = jnp.take_along_axis(cache_slot.reshape(owner_count, requests), which_req, axis=1)
    outgoing = jnp.where(present[:, :, None, None, None], cache_states[wanted], 0.0)
    incoming = lax.all_to_all(
        outgoing.astype(jnp.bfloat16), "req", split_axis=0, concat_axis=0, tiled=True
    ).astype(outgoing.dtype)
    start_state = incoming[my_owner, my_rank]
    query_scale = key_width ** (-0.5)
    query_short = (jnp.repeat(unit_rows(queries), repeats, axis=1) * query_scale).astype(
        jnp.bfloat16
    )
    key_short = jnp.repeat(unit_rows(key_rows), repeats, axis=1).astype(jnp.bfloat16)
    query_all = arrange(query_short, requests)
    key_all = arrange(key_short, requests)
    value_all = arrange(values, requests)
    rate_all = arrange(write_rate, requests)
    decay_all = arrange(log_decay, requests)
    inputs_all = (query_all, key_all, value_all, rate_all, decay_all)

    def block_parts(block_idx):
        return prepare(
            *(
                lax.dynamic_index_in_dim(part_arr, block_idx, axis=2, keepdims=False)
                for part_arr in inputs_all
            )
        )

    last_block = my_blocks - 1

    def advance_block(block_idx, carry_all):
        carried, outputs, final_state = carry_all
        block_out, carried = advance(carried, *block_parts(block_idx))
        outputs = lax.dynamic_update_index_in_dim(outputs, block_out, block_idx, 2)
        final_state = jnp.where(
            (last_block == block_idx)[:, None, None, None], carried, final_state
        )
        return (carried, outputs, final_state)

    outputs = jnp.zeros(value_all.shape, jnp.float32)
    carried, outputs, final_state = lax.fori_loop(
        0, jnp.max(my_blocks), advance_block, (start_state, outputs, jnp.zeros_like(start_state))
    )
    token_out = jnp.transpose(outputs, (0, 2, 3, 1, 4)).reshape(values.shape)
    positions = jnp.arange(TAIL_POSITIONS, dtype=jnp.int32)
    live_mask = (positions[None, :] < (my_blocks * BLOCK)[:, None]).reshape(-1)
    spread = jnp.mean(token_out * token_out, axis=-1, keepdims=True)
    normed = (
        token_out
        * lax.rsqrt(spread + EPSILON)
        * norm_gain
        * jax.nn.silu(gate_input.astype(jnp.float32))
    )
    normed = (
        jnp.where(live_mask[:, None, None], normed, 0.0)
        .astype(jnp.bfloat16)
        .reshape(values.shape[0], -1)
    )
    layer_out = lax.psum_scatter(
        jnp.dot(normed, out_weight, preferred_element_type=jnp.float32).astype(jnp.bfloat16),
        "head",
        scatter_dimension=0,
        tiled=True,
    )
    owner_ids = jnp.arange(owner_count, dtype=jnp.int32)
    send_match = (my_owner[None, None, :] == owner_ids[:, None, None]) & (
        my_rank[None, None, :] == pair_ids[None, :, None]
    )
    send_present = jnp.any(send_match, axis=2)
    send_which = jnp.sum(jnp.where(send_match, request_ids, 0), axis=2)
    leaving = jnp.where(send_present[:, :, None, None, None], final_state[send_which], 0.0)
    arriving = lax.all_to_all(
        leaving.astype(jnp.bfloat16), "req", split_axis=0, concat_axis=0, tiled=True
    ).astype(leaving.dtype)
    slot_table = jnp.take_along_axis(new_slot.reshape(owner_count, requests), which_req, axis=1)
    slot_ids = jnp.arange(requests, dtype=jnp.int32)
    claimed = present[None] & (slot_table[None] == slot_ids[:, None, None])
    flat_ids = jnp.arange(owner_count * pair_cap, dtype=jnp.int32).reshape(owner_count, pair_cap)
    source_row = jnp.sum(jnp.where(claimed, flat_ids[None], 0), axis=(1, 2))
    new_cache = arriving.reshape((owner_count * pair_cap,) + arriving.shape[2:])[source_row]
    return (layer_out, new_cache)


def solution(mesh):
    return jax.shard_map(
        local,
        mesh=mesh,
        in_specs=(
            P("req", "head", None),
            P("req", "head", None),
            P("req", "head", None),
            P("req", "head", None),
            P("req", "head"),
            P("req", "head"),
            P(),
            P("head", None),
            P("req", "head", None, None),
            P(),
            P(),
            P(),
            P(),
        ),
        out_specs=(P(("req", "head"), None), P("req", "head", None, None)),
        check_vma=False,
    )
```

profile of v0, /device:TPU:0, one launch (start us, length us, event | category | flops | bytes accessed | tf_op | source)
XLA Modules:
  0.0 1353.4 jit_solution(6383140403372271221)
XLA Ops:
  16.8 6.1 fusion.39
  22.8 8.5 all-to-all-start
  32.6 6.3 fusion.48
  39.2 7.2 fusion.49
  47.7 5.2 fusion.50
  53.2 7.3 fusion.52
  67.2 17.7 %all-to-all-done = bf16[32,1,4,128,128]{4,3,2,1,0:T(8,128)(2,1)} async-done(((bf16[32,1,4,128,128]{4,3,2,1,0:T(8,128)(2,1)}), bf16[32,1,4,128,128]{4,3,2,1,0:T(8,128)(2,1)}, u32[]{:S(2)}, u32[]{:S(2)}) %all-to-all-start) | async-done | bytes 4194336 | tf_op jit(solution)/shard_map/all_to_all | solution.py:119
  84.9 6.5 convert_element_type.88
  91.4 7.2 gather_fusion.1
  110.1 1096.6 %while.14 = (s32[]{:T(128)}, f32[24,4,128,128]{3,2,1,0:T(8,128)}, f32[24,4,2,64,128]{4,3,2,0,1:T(8,128)}, bf16[24,4,128,128]{3,2,1,0:T(8,128)(2,1)}, s32[]{:T(12...) while((s32[]{:T(128)}, f32[24,4,128,128]{3,2,1,0:T(8,128)}, ...), condition=%wide.region_9.11_spmd, body=%wide.region_7.10_spmd.sunk | while | flops 5656446976 | bytes 213258352 | solution.py:155
  139.0 473.3 %custom-call.18 = f32[24,4,1,64,64]{3,4,2,1,0:T(8,128)} custom-call(f32[24,4,1,64,64]{4,3,2,1,0:T(8,128)} %fusion.108), custom_call_target="InvertDiagBlocksLowerTriangular" | custom-call | tf_op jit(solution)/shard_map/while/body/triangular_solve | solution.py:45
  619.1 6.5 fusion.109
  625.6 6.4 slice_subtract_fusion.2
  633.6 4.6 fusion.111
  638.2 6.5 add_bitcast_fusion.3
  648.0 17.8 %broadcast_select_fusion.2 = (bf16[24,4,128,128]{3,2,1,0:T(8,128)(2,1)}, f32[24,4,128,128]{3,2,1,0:T(8,128)}) fusion(bf16[24,4,128,128]{3,2,1,0:T(8,128)(2,1)} %get-tuple-element.264, pred[24]{0:T(512)(128)(4,1)S(1)} %broadcast_compare_fusion.5, f32[24,4,64,128]{3,2,1,0:T(8,128)} %copy-done.1, f32[24,4,64]{2,1,0:T(4,128)S(1)} %copy.161, ...), kind=kOutput, calls=%fused_computation.37.clone.1 | convolution fusion | flops 1214251008 | bytes 23617948 | tf_op jit(solution)/shard_map/while/body/...tk,...tv->...kv/dot_general | solution.py:69
  672.1 473.3 %custom-call.18 = f32[24,4,1,64,64]{3,4,2,1,0:T(8,128)} custom-call(f32[24,4,1,64,64]{4,3,2,1,0:T(8,128)} %fusion.108), custom_call_target="InvertDiagBlocksLowerTriangular" | custom-call | tf_op jit(solution)/shard_map/while/body/triangular_solve | solution.py:45
  1152.1 6.5 fusion.109
  1158.6 6.4 slice_subtract_fusion.2
  1166.7 4.6 fusion.111
  1171.3 6.5 add_bitcast_fusion.3
  1181.0 17.8 %broadcast_select_fusion.2 = (bf16[24,4,128,128]{3,2,1,0:T(8,128)(2,1)}, f32[24,4,128,128]{3,2,1,0:T(8,128)}) fusion(bf16[24,4,128,128]{3,2,1,0:T(8,128)(2,1)} %get-tuple-element.264, pred[24]{0:T(512)(128)(4,1)S(1)} %broadcast_compare_fusion.5, f32[24,4,64,128]{3,2,1,0:T(8,128)} %copy-done.1, f32[24,4,64]{2,1,0:T(4,128)S(1)} %copy.161, ...), kind=kOutput, calls=%fused_computation.37.clone.1 | convolution fusion | flops 1214251008 | bytes 23617948 | tf_op jit(solution)/shard_map/while/body/...tk,...tv->...kv/dot_general | solution.py:69
  1211.5 7.7 fusion.47
  1219.1 4.6 copy.103
  1223.8 11.5 convolution_convert_fusion
  1236.2 5.4 gather_fusion.2
  1241.6 6.2 fusion.38
  1247.9 5.0 all-to-all-start.1
  1253.0 53.3 %all-to-all-done.1 = bf16[32,1,4,128,128]{4,3,2,1,0:T(8,128)(2,1)} async-done(((bf16[32,1,4,128,128]{4,3,2,1,0:T(8,128)(2,1)}), bf16[32,1,4,128,128]{4,3,2,1,0:T(8,128)(2,1)}, u32[]{:S(2)}, u32[]{:S(2)}) %all-to-all-start.1) | async-done | bytes 4194336 | tf_op jit(solution)/shard_map/all_to_all | solution.py:186
  1306.3 6.5 bitcast_convert_fusion
  1312.8 7.1 gather_fusion.3
  1319.9 26.5 %reduce-scatter.2.cloned.1.call-done = bf16[768,2048]{1,0:T(8,128)(2,1)} async-done(((bf16[3072,2048]{1,0:T(8,128)(2,1)}), bf16[768,2048]{1,0:T(8,128)(2,1)}) %reduce-scatter.2.cloned.1.call-update) | async-done | bytes 3145744 | tf_op jit(solution)/shard_map/reduce_scatter | solution.py:173
  (162 shorter events, 70.9 us)
Async XLA Ops:
  7.2 1216.6 %copy-start = (bf16[512,2048]{1,0:T(8,128)(2,1)S(1)}, bf16[512,2048]{1,0:T(8,128)(2,1)}, u32[]{:S(2)}) copy-start(bf16[512,2048]{1,0:T(8,128)(2,1)} %param.24) | copy-start | bytes 6291460
  8.5 8.3 copy-start.13
  22.8 62.0 %all-to-all-start = ((bf16[32,1,4,128,128]{4,3,2,1,0:T(8,128)(2,1)}), bf16[32,1,4,128,128]{4,3,2,1,0:T(8,128)(2,1)}, u32[]{:S(2)}, u32[]{:S(2)}) async-start(bf16[32,1,4,128,128]{4,3,2,1,0:T(8,128)(2,1)} %fusion.39), calls=%async_computation | async-start | bytes 8388608 | tf_op jit(solution)/shard_map/all_to_all | solution.py:119
  31.4 1315.0 %reduce-scatter.2.cloned.1.call-start = ((), (), s32[]{:S(2)}) async-start(), calls=%async_computation.3 | async-start | bytes 15728640 | tf_op jit(solution)/shard_map/reduce_scatter | solution.py:173
  32.6 33.0 %copy-start.19 = (s32[24]{0:T(128)}, s32[24]{0:T(128)S(1)}, u32[]{:S(2)}) copy-start(s32[24]{0:T(128)S(1)} %dynamic_slice.24) | copy-start | bytes 292
  32.6 6.6 copy-start.6
  39.2 8.6 copy-start.7
  53.2 8.7 copy-start.9
  61.9 2.0 copy-start.10
  61.9 2.2 copy-start.11
  65.7 25.6 %copy-start.17 = (s32[24]{0:T(128)}, s32[24]{0:T(128)S(1)}, u32[]{:S(2)}) copy-start(s32[24]{0:T(128)S(1)} %convert_reduce_fusion) | copy-start | bytes 292
  98.5 3.6 copy-start.8
  612.3 2.6 copy-start.5
  617.2 1.9 copy-start.3
  617.2 8.4 slice-start
  619.1 6.5 slice-start.1
  625.5 6.4 copy-start.2
  633.6 11.2 slice-start.2
  638.2 6.6 slice-start.3
  645.2 2.6 copy-start.4
  1145.4 2.6 copy-start.5
  1150.3 8.4 slice-start
  1152.1 6.5 slice-start.1
  1158.6 6.4 copy-start.2
  1166.7 11.2 slice-start.2
  1171.3 6.6 slice-start.3
  1178.3 2.6 copy-start.4
  1206.7 4.8 copy-start.12
  1206.7 4.8 copy-start.15
  1247.9 5.0 copy-start.14
  1247.9 5.0 copy-start.16
  1247.9 58.5 %all-to-all-start.1 = ((bf16[32,1,4,128,128]{4,3,2,1,0:T(8,128)(2,1)}), bf16[32,1,4,128,128]{4,3,2,1,0:T(8,128)(2,1)}, u32[]{:S(2)}, u32[]{:S(2)}) async-start(bf16[32,1,4,128,128]{4,3,2,1,0:T(8,128)(2,1)} %fusion.38), calls=%async_computation.2 | async-start | bytes 8388608 | tf_op jit(solution)/shard_map/all_to_all | solution.py:186
  (5 other events, 6.5 us)
Sparse Core Ops, SparseCore 0:
  1235.4 110.8 reduce-scatter.1
where the time goes:
time: 1360 us; the launch traced here: 1350 us
  other arithmetic  1020 us (75%)
  matrix products  106 us (8%)
  waiting for transfers between devices  97.5 us (7%)
  local copies, waits for them, and re-layouts  64.9 us (5%)
  loops' own time  32.1 us (2%)
  between operations  14.5 us (1%)
  starting transfers between devices  13.9 us (1%)
    another operation x4, other arithmetic, prepare(): lax.linalg.triangular_solve(system, targets, left_side=True, lower=True,...  947 us
    all_to_all x1, waiting for transfers between devices, local(): lax.all_to_all(leaving.astype(jnp.bfloat16), 'req', split_axis=0, concat_...  53.3 us
    dot_general x2, matrix products, advance(): jnp.einsum('...tk,...tv->...kv', key_fade, fresh_values, precision=HIGHEST)  35.7 us
    another operation x1, loops' own time, local(): lax.fori_loop(0, jnp.max(my_blocks), advance_block, (start_state, outputs...  32.1 us
  transfers between devices with their start and end apart: 3, of which 3 were waited for; matrix products, arithmetic and copies ran while one was open for 4% of the time, Pallas kernels for 0%

commit v1 on v0

v1 whole, which is shorter than its diff:
```python
import functools

import jax
import jax.numpy as jnp
from jax import lax
from jax.experimental import pallas as pl
from jax.experimental.pallas import tpu as pltpu
from jax.sharding import PartitionSpec as P

BLOCK = 64
TAIL_POSITIONS = 128
WIDTH = 128
BASE = 16
EPSILON = 1e-06
HIGHEST = lax.Precision.HIGHEST
BF16 = jnp.bfloat16
F32 = jnp.float32
VMEM_LIMIT = 56 * 1024 * 1024


def iota(shape, dim):
    return lax.broadcasted_iota(jnp.int32, shape, dim)


def dot(left, right, dims=((1,), (0,))):
    return lax.dot_general(left, right, (dims, ((), ())), preferred_element_type=F32)


def params(**kwargs):
    return pltpu.CompilerParams(vmem_limit_bytes=VMEM_LIMIT, **kwargs)


def pick_kernel(per_step, slot_ref, cache_ref, out_ref):
    step = pl.program_id(0)
    for i in range(per_step):
        out_ref[i] = cache_ref[slot_ref[step * per_step + i]].astype(BF16)


def pick_states(wanted, cache_states, chunk, heads):
    slots = cache_states.shape[0]
    count = wanted.shape[0]
    per_step = min(8, count)
    return pl.pallas_call(
        functools.partial(pick_kernel, per_step),
        out_shape=jax.ShapeDtypeStruct((count, heads, WIDTH, WIDTH), BF16),
        grid_spec=pltpu.PrefetchScalarGridSpec(
            num_scalar_prefetch=1,
            grid=(count // per_step,),
            in_specs=[
                pl.BlockSpec((slots, heads, WIDTH, WIDTH), lambda s, _: (0, chunk, 0, 0))
            ],
            out_specs=pl.BlockSpec(
                (per_step, heads, WIDTH, WIDTH), lambda s, _: (s, 0, 0, 0)
            ),
        ),
        compiler_params=params(),
        cost_estimate=pl.CostEstimate(
            flops=0, bytes_accessed=6 * count * heads * WIDTH * WIDTH, transcendentals=0
        ),
        name="pick_states",
    )(wanted, cache_states)


def unit_rows(vectors):
    vectors = vectors.astype(F32)
    return vectors * lax.rsqrt(
        jnp.sum(vectors * vectors, axis=-1, keepdims=True) + EPSILON
    )


def unit_lower_inverse(systems):
    count = len(systems)
    shape = (TAIL_POSITIONS, TAIL_POSITIONS)
    row, col = iota(shape, 0), iota(shape, 1)
    parts = TAIL_POSITIONS // BASE
    diagonal = (row // BASE) == (col // BASE)
    packed = []
    for system in systems:
        inner = jnp.where(diagonal, system, 0.0)
        total = inner[:BASE]
        for part in range(1, parts):
            total = total + inner[part * BASE : (part + 1) * BASE]
        packed.append(total)
    short = (BASE, TAIL_POSITIONS)
    lane = iota(short, 1)
    first = jnp.where(iota(short, 0) == lane % BASE, 1.0, 0.0)
    solved = [first] * count
    for step in range(BASE - 1):
        index = (lane // BASE) * BASE + step
        for i in range(count):
            factor = jnp.take_along_axis(packed[i], index, axis=1)
            solved[i] = solved[i] - factor * solved[i][step : step + 1]
    inverses = [
        jnp.where(diagonal, jnp.concatenate([x] * parts, axis=0), 0.0) for x in solved
    ]
    size = BASE
    while size < TAIL_POSITIONS:
        if size * 2 < TAIL_POSITIONS:
            below = ((row // (2 * size)) == (col // (2 * size))) & (
                (row // size) != (col // size)
            )
            short_inv = [x.astype(BF16) for x in inverses]
            moved = [
                dot(jnp.where(below, system, 0.0).astype(BF16), x).astype(BF16)
                for system, x in zip(systems, short_inv)
            ]
            inverses = [
                x - dot(s, m) for x, s, m in zip(inverses, short_inv, moved)
            ]
        else:
            short_inv = [x.astype(BF16) for x in inverses]
            moved = [
                dot(system[size:, :size].astype(BF16), x[:size, :size]).astype(BF16)
                for system, x in zip(systems, short_inv)
            ]
            corner = [dot(x[size:, size:], m) for x, m in zip(short_inv, moved)]
            inverses = [
                jnp.concatenate(
                    [x[:size], jnp.concatenate([-c, x[size:, size:]], axis=1)], axis=0
                )
                for x, c in zip(inverses, corner)
            ]
        size *= 2
    return inverses


def prep_kernel(per_step, blocks_ref, q_ref, k_ref, v_ref, rows_ref, maps_ref, own_ref):
    step = pl.program_id(0)
    tokens = TAIL_POSITIONS
    square = (tokens, tokens)
    row, col = iota(square, 0), iota(square, 1)
    upto = jnp.where(row <= col, 1.0, 0.0)
    within = row >= col
    strict = row > col
    scale = WIDTH ** (-0.5)

    masked = []
    for r in range(per_step):
        live = iota((4, tokens), 1) < blocks_ref[step * per_step + r] * BLOCK
        masked.append(jnp.where(live, rows_ref[0, :, r * tokens : (r + 1) * tokens], 0.0))
    masked = jnp.concatenate(masked, axis=0)
    running = lax.dot_general(
        masked, upto, (((1,), (0,)), ((), ())), precision=HIGHEST, preferred_element_type=F32
    )
    tall = jnp.transpose(jnp.concatenate([masked, running], axis=0))

    keys, queries, systems, fades, scores = [], [], [], [], []
    for r in range(per_step):
        span = pl.ds(r * tokens, tokens)
        k = unit_rows(k_ref[span, :]).astype(BF16)
        q = (unit_rows(q_ref[span, :]) * scale).astype(BF16)
        keys.append(k)
        queries.append(q)
        pair = dot(jnp.concatenate([k, q], axis=0), k, ((1,), (1,)))
        for h in range(2):
            at = r * 4 + 2 + h
            run_row = running[at : at + 1]
            run_col = tall[:, per_step * 4 + at : per_step * 4 + at + 1]
            rate_col = tall[:, r * 4 + h : r * 4 + h + 1]
            fade = jnp.exp(jnp.where(within, run_col - run_row, -1e30))
            systems.append(jnp.where(strict, rate_col * pair[:tokens] * fade, 0.0))
            scores.append((pair[tokens:] * fade).astype(BF16))
    inverses = unit_lower_inverse(systems)
    solved = []
    for r in range(per_step):
        key_wide = keys[r].astype(F32)
        for h in range(2):
            i = r * 2 + h
            at = r * 4 + 2 + h
            grow_col = jnp.exp(tall[:, per_step * 4 + at : per_step * 4 + at + 1])
            rate_row = masked[r * 4 + h : r * 4 + h + 1]
            left = (inverses[i] * rate_row).astype(BF16)
            right = jnp.concatenate(
                [
                    v_ref[pl.ds(r * tokens, tokens), h * WIDTH : (h + 1) * WIDTH],
                    (key_wide * grow_col).astype(BF16),
                ],
                axis=1,
            )
            solved.append(dot(left, right).astype(BF16))
    for r in range(per_step):
        key_turned = jnp.transpose(keys[r].astype(F32))
        query_wide = queries[r].astype(F32)
        for h in range(2):
            i = r * 2 + h
            at = r * 4 + 2 + h
            run_row = running[at : at + 1]
            end = run_row[:, tokens - 1 : tokens]
            grow_col = jnp.exp(tall[:, per_step * 4 + at : per_step * 4 + at + 1])
            ending = (key_turned * jnp.exp(end - run_row)).astype(BF16)
            both = dot(jnp.concatenate([scores[i], ending], axis=0), solved[i])
            own_ref[r, h] = both[:, :WIDTH].astype(BF16)
            kept = jnp.where(row == col, jnp.exp(end), 0.0)
            maps_ref[r, h, :tokens] = (query_wide * grow_col - both[:tokens, WIDTH:]).astype(BF16)
            maps_ref[r, h, tokens:] = (kept - both[tokens:, WIDTH:]).astype(BF16)


def prepare(blocks, queries, keys, values, rows, chunk):
    requests = blocks.shape[0]
    per_step = 4
    span = per_step * TAIL_POSITIONS
    tall = (requests, 2, TAIL_POSITIONS + WIDTH, WIDTH)
    block = pl.BlockSpec((per_step,) + tall[1:], lambda s, _: (s, 0, 0, 0))
    return pl.pallas_call(
        functools.partial(prep_kernel, per_step),
        out_shape=(jax.ShapeDtypeStruct(tall, BF16), jax.ShapeDtypeStruct(tall, BF16)),
        grid_spec=pltpu.PrefetchScalarGridSpec(
            num_scalar_prefetch=1,
            grid=(requests // per_step,),
            in_specs=[
                pl.BlockSpec((span, WIDTH), lambda s, _: (s, chunk)),
                pl.BlockSpec((span, WIDTH), lambda s, _: (s, chunk)),
                pl.BlockSpec((span, 2 * WIDTH), lambda s, _: (s, chunk)),
                pl.BlockSpec((1, 4, span), lambda s, _: (chunk, 0, s)),
            ],
            out_specs=(block, block),
        ),
        compiler_params=params(),
        cost_estimate=pl.CostEstimate(
            flops=requests * 2 * 24 * 2 * 128**3, bytes_accessed=24 << 20, transcendentals=0
        ),
        name="prepare",
    )(blocks, queries, keys, values, rows)


def advance_kernel(
    per_step, owner_ref, blocks_ref, state_ref, maps_ref, own_ref, gate_ref, gain_ref, normed_ref, final_ref
):
    step = pl.program_id(0)
    tokens = TAIL_POSITIONS
    gain = gain_ref[...]
    for r in range(per_step):
        request = step * per_step + r
        owner = owner_ref[request]
        live = iota((tokens, WIDTH), 0) < blocks_ref[request] * BLOCK
        for h in range(2):
            both = dot(maps_ref[r, h], state_ref[owner, h]) + own_ref[r, h].astype(F32)
            final_ref[owner, h] = both[tokens:].astype(BF16)
            core = both[:tokens]
            gate = gate_ref[pl.ds(r * tokens, tokens), h * WIDTH : (h + 1) * WIDTH].astype(F32)
            spread = jnp.mean(core * core, axis=-1, keepdims=True)
            normed = core * lax.rsqrt(spread + EPSILON) * gain * (gate / (1.0 + jnp.exp(-gate)))
            normed_ref[pl.ds(r * tokens, tokens), h * WIDTH : (h + 1) * WIDTH] = jnp.where(
                live, normed, 0.0
            ).astype(BF16)


def advance(owners, blocks, states, maps, own, gates, gain, chunk):
    requests = blocks.shape[0]
    per_step = 4
    span = per_step * TAIL_POSITIONS
    tall = (per_step, 2, TAIL_POSITIONS + WIDTH, WIDTH)
    whole = pl.BlockSpec(states.shape, lambda s, *_: (0, 0, 0, 0))
    return pl.pallas_call(
        functools.partial(advance_kernel, per_step),
        out_shape=(
            jax.ShapeDtypeStruct((requests * TAIL_POSITIONS, 2 * WIDTH), BF16),
            jax.ShapeDtypeStruct(states.shape, BF16),
        ),
        grid_spec=pltpu.PrefetchScalarGridSpec(
            num_scalar_prefetch=2,
            grid=(requests // per_step,),
            in_specs=[
                whole,
                pl.BlockSpec(tall, lambda s, *_: (s, 0, 0, 0)),
                pl.BlockSpec(tall, lambda s, *_: (s, 0, 0, 0)),
                pl.BlockSpec((span, 2 * WIDTH), lambda s, *_: (s, chunk)),
                pl.BlockSpec((1, WIDTH), lambda s, *_: (0, 0)),
            ],
            out_specs=(
                pl.BlockSpec((span, 2 * WIDTH), lambda s, *_: (s, 0)),
                whole,
            ),
        ),
        compiler_params=params(),
        cost_estimate=pl.CostEstimate(
            flops=requests * 2 * 4 * 128**3, bytes_accessed=16 << 20, transcendentals=0
        ),
        name="advance",
    )(owners, blocks, states, maps, own, gates, gain)


def place_kernel(per_step, source_ref, arrived_ref, *refs):
    out_ref = refs[-1]
    step = pl.program_id(0)
    for i in range(per_step):
        out_ref[i] = arrived_ref[source_ref[step * per_step + i]].astype(F32)


def place(source, arrived, earlier, chunk, heads_all):
    slots = source.shape[0]
    heads = arrived.shape[1]
    per_step = 4
    operands = [source, arrived]
    in_specs = [pl.BlockSpec(arrived.shape, lambda s, _: (0, 0, 0, 0))]
    aliases = {}
    if earlier is not None:
        operands.append(earlier)
        in_specs.append(pl.BlockSpec(memory_space=pl.ANY))
        aliases = {2: 0}
    return pl.pallas_call(
        functools.partial(place_kernel, per_step),
        out_shape=jax.ShapeDtypeStruct((slots, heads_all, WIDTH, WIDTH), F32),
        grid_spec=pltpu.PrefetchScalarGridSpec(
            num_scalar_prefetch=1,
            grid=(slots // per_step,),
            in_specs=in_specs,
            out_specs=pl.BlockSpec(
                (per_step, heads, WIDTH, WIDTH), lambda s, _: (s, chunk, 0, 0)
            ),
        ),
        input_output_aliases=aliases,
        compiler_params=params(),
        cost_estimate=pl.CostEstimate(flops=0, bytes_accessed=5 << 20, transcendentals=0),
        name="place",
    )(*operands)


def project_kernel(groups, *refs):
    *arrived, weight_ref, out_ref = refs
    chunks = len(arrived)
    width = arrived[0].shape[2]
    total = None
    for group in range(groups):
        for chunk in range(chunks):
            first = (group * chunks + chunk) * width
            term = dot(arrived[chunk][group], weight_ref[pl.ds(first, width), :])
            total = term if total is None else total + term
    out_ref[...] = total.astype(BF16)


def project(arrived, weight):
    groups, rows, width = arrived[0].shape
    model = weight.shape[1]
    tile = 256
    return pl.pallas_call(
        functools.partial(project_kernel, groups),
        out_shape=jax.ShapeDtypeStruct((rows, model), BF16),
        grid=(model // tile,),
        in_specs=[
            pl.BlockSpec(a.shape, lambda n: (0, 0, 0), pipeline_mode=pl.Buffered(1))
            for a in arrived
        ]
        + [pl.BlockSpec((weight.shape[0], tile), lambda n: (0, n))],
        out_specs=pl.BlockSpec((rows, tile), lambda n: (0, n)),
        compiler_params=params(),
        cost_estimate=pl.CostEstimate(
            flops=2 * rows * weight.shape[0] * model, bytes_accessed=16 << 20, transcendentals=0
        ),
        name="project",
    )(*arrived, weight)


def local(
    queries,
    key_rows,
    values,
    gate_input,
    write_rate,
    log_decay,
    norm_gain,
    out_weight,
    cache_states,
    cache_owner,
    cache_slot,
    suffix_blocks,
    new_slot,
):
    owner_count = lax.axis_size("req")
    groups = lax.axis_size("head")
    device = lax.axis_index("req")
    tokens = queries.shape[0]
    requests = tokens // TAIL_POSITIONS
    heads_all = values.shape[1]
    chunks = queries.shape[1]
    heads = heads_all // chunks

    naming = cache_owner.reshape(owner_count, requests) == device
    wanted = jnp.sum(jnp.where(naming, cache_slot.reshape(owner_count, requests), 0), axis=1)
    picked = [pick_states(wanted, cache_states, c, heads) for c in range(chunks)]
    arrived = [
        lax.all_to_all(p, "req", split_axis=0, concat_axis=0, tiled=True) for p in picked
    ]
    weight = lax.all_gather(out_weight, "head", axis=0, tiled=True)

    my_owner = lax.dynamic_slice_in_dim(cache_owner, device * requests, requests)
    my_blocks = lax.dynamic_slice_in_dim(suffix_blocks, device * requests, requests)
    slot_ids = jnp.arange(requests, dtype=jnp.int32)
    claimed = naming[None] & (
        new_slot.reshape(owner_count, requests)[None] == slot_ids[:, None, None]
    )
    device_ids = jnp.arange(owner_count, dtype=jnp.int32)[None, :, None]
    source = jnp.sum(jnp.where(claimed, device_ids, 0), axis=(1, 2))

    query_flat = queries.reshape(tokens, -1)
    key_flat = key_rows.reshape(tokens, -1)
    value_flat = values.reshape(tokens, -1)
    gate_flat = gate_input.reshape(tokens, -1)
    rows = jnp.concatenate(
        [
            write_rate.T.reshape(chunks, heads, tokens),
            log_decay.T.reshape(chunks, heads, tokens),
        ],
        axis=1,
    )
    gain = norm_gain.reshape(1, -1)

    leaving, shares = [], []
    ready = [
        prepare(my_blocks, query_flat, key_flat, value_flat, rows, c) for c in range(chunks)
    ]
    for c in range(chunks):
        normed, final = advance(my_owner, my_blocks, arrived[c], *ready[c], gate_flat, gain, c)
        leaving.append(lax.all_to_all(final, "req", split_axis=0, concat_axis=0, tiled=True))
        shares.append(
            lax.all_to_all(
                normed.reshape(groups, tokens // groups, heads * WIDTH),
                "head",
                split_axis=0,
                concat_axis=0,
                tiled=True,
            )
        )
    layer_out = project(shares, weight)
    new_cache = None
    for c in range(chunks):
        new_cache = place(source, leaving[c], new_cache, c, heads_all)
    return (layer_out, new_cache)


def solution(mesh):
    return jax.shard_map(
        local,
        mesh=mesh,
        in_specs=(
            P("req", "head", None),
            P("req", "head", None),
            P("req", "head", None),
            P("req", "head", None),
            P("req", "head"),
            P("req", "head"),
            P(),
            P("head", None),
            P("req", "head", None, None),
            P(),
            P(),
            P(),
            P(),
        ),
        out_specs=(P(("req", "head"), None), P("req", "head", None, None)),
        check_vma=False,
    )
```

time: 1360 us -> 252 us (0.19)
  other arithmetic: 1020 us -> 2.37 us
  matrix products: 106 us -> 0 us
  Pallas kernels: 0 us -> 92 us
  blocking collectives: 0 us -> 68.4 us
  waiting for transfers between devices: 97.5 us -> 36.5 us
  local copies, waits for them, and re-layouts: 64.9 us -> 15.7 us
  loops' own time: 32.1 us -> 0 us
    another operation x8 -> x0, other arithmetic: 949 us -> none  [the longest x4 947 us: prepare(): lax.linalg.triangular_solve(system, targets, left_side=True, lower=True,...]
    dot_general x13 -> x0, matrix products: 93.3 us -> none  [the longest x2 35.7 us: advance(): jnp.einsum('...tk,...tv->...kv', key_fade, fresh_values, precision=HIGHEST)]
    pallas_call x0 -> x9, Pallas kernels: none -> 92 us  [the longest x2 43.3 us: prepare(): pl.pallas_call(functools.partial(prep_kernel, per_step), out_shape=(jax.S...]
    all_to_all x0 -> x2, blocking collectives: none -> 68.4 us  [local(): lax.all_to_all(final, 'req', split_axis=0, concat_axis=0, tiled=True)]
    convert_element_type x9 -> x0, other arithmetic: 41.8 us -> none  [the longest x1 7.68 us: local(): normed = jnp.where(live_mask[:, None, None], normed, 0.0).astype(jnp.bflo...]
    all_to_all x2 -> x4, waiting for transfers between devices: 71 us -> 35.9 us  [the longest x2 26 us: local(): lax.all_to_all(p, 'req', split_axis=0, concat_axis=0, tiled=True)]
    another operation x1 -> x0, loops' own time: 32.1 us -> none  [local(): lax.fori_loop(0, jnp.max(my_blocks), advance_block, (start_state, outputs...]
    reduce_scatter x1 -> x0, waiting for transfers between devices: 26.5 us -> none  [local(): lax.psum_scatter(jnp.dot(normed, out_weight, preferred_element_type=jnp.f...]
  transfers between devices with their start and end apart: 3 -> 5, of which waited for: 3 -> 2; matrix products, arithmetic and copies ran while one was open for 4% -> 6% of each run, Pallas kernels for 0% -> 32%
where the time goes in v1:
time: 252 us; the launch traced here: 251 us
  Pallas kernels  92 us (37%)
  blocking collectives  68.4 us (27%)
  waiting for transfers between devices  36.5 us (14%)
  starting transfers between devices  21.7 us (9%)
  local copies, waits for them, and re-layouts  15.7 us (6%)
  between operations  14.2 us (6%)
    all_to_all x2, blocking collectives, local(): lax.all_to_all(final, 'req', split_axis=0, concat_axis=0, tiled=True)  68.4 us
    pallas_call x2, Pallas kernels, prepare(): pl.pallas_call(functools.partial(prep_kernel, per_step), out_shape=(jax.S...  43.3 us
    all_to_all x2, waiting for transfers between devices, local(): lax.all_to_all(p, 'req', split_axis=0, concat_axis=0, tiled=True)  26 us
    pallas_call x2, Pallas kernels, advance(): pl.pallas_call(functools.partial(advance_kernel, per_step), out_shape=(ja...  18.8 us
    all_to_all x2, starting transfers between devices, local(): lax.all_to_all(p, 'req', split_axis=0, concat_axis=0, tiled=True)  12.4 us
    pallas_call x1, Pallas kernels, project(): pl.pallas_call(functools.partial(project_kernel, groups), out_shape=jax.S...  12.3 us
    unnamed x24, local copies, waits for them, and re-layouts  11.1 us
    pallas_call x2, Pallas kernels, place(): pl.pallas_call(functools.partial(place_kernel, per_step), out_shape=jax.S...  9.86 us
  transfers between devices with their start and end apart: 5, of which 2 were waited for; matrix products, arithmetic and copies ran while one was open for 6% of the time, Pallas kernels for 32%

profile of v1, /device:TPU:0, one launch (start us, length us, event | category | flops | bytes accessed | tf_op | source)
XLA Modules:
  0.0 251.0 jit_solution(16993112243891342419)
XLA Ops:
  7.2 0.7 all-gather.2.cloned.1.call-update
  7.9 0.1 eq.30
  8.1 0.1 reshape.43
  8.1 0.6 select_reduce_fusion.1.slot_ref
  8.8 3.8 %pick_states.2 = bf16[32,2,128,128]{3,2,1,0:T(8,128)(2,1)} custom-call(s32[32]{0:T(128)} %select_reduce_fusion.1.slot_ref, f32[8,4,128,128]{3,2,1,0:T(8,128)} %cache_ref.3), custom_call_target="tpu_custom_call" | custom-call | bytes 6291456 | tf_op jit(solution)/shard_map/pick_states/pallas_call | solution.py:43
  12.5 8.4 %all-to-all-start = ((bf16[32,2,128,128]{3,2,1,0:T(8,128)(2,1)}), bf16[32,2,128,128]{3,2,1,0:T(8,128)(2,1)S(1)}, u32[]{:S(2)}, u32[]{:S(2)}) async-start(bf16[32,2,128,128]{3,2,1,0:T(8,128)(2,1)} %pick_states.2), calls=%async_computation | async-start | bytes 4194304 | tf_op jit(solution)/shard_map/all_to_all | solution.py:382
  21.0 4.0 %pick_states.3 = bf16[32,2,128,128]{3,2,1,0:T(8,128)(2,1)} custom-call(s32[32]{0:T(128)} %select_reduce_fusion.1.slot_ref, f32[8,4,128,128]{3,2,1,0:T(8,128)} %cache_ref.3), custom_call_target="tpu_custom_call" | custom-call | bytes 6291456 | tf_op jit(solution)/shard_map/pick_states/pallas_call | solution.py:43
  24.9 26.0 %all-to-all-done.state_ref = bf16[32,2,128,128]{3,2,1,0:T(8,128)(2,1)S(1)} async-done(((bf16[32,2,128,128]{3,2,1,0:T(8,128)(2,1)}), bf16[32,2,128,128]{3,2,1,0:T(8,128)(2,1)S(1)}, u32[]{:S(2)}, u32[]{:S(2)}) %all-to-all-start) | async-done | bytes 2097184 | tf_op jit(solution)/shard_map/all_to_all | solution.py:382
  51.0 1.3 copy-done.1
  52.3 4.0 %all-to-all-start.2 = ((bf16[32,2,128,128]{3,2,1,0:T(8,128)(2,1)}), bf16[32,2,128,128]{3,2,1,0:T(8,128)(2,1)S(1)}, u32[]{:S(2)}, u32[]{:S(2)}) async-start(bf16[32,2,128,128]{3,2,1,0:T(8,128)(2,1)} %pick_states.3), calls=%async_computation.2 | async-start | bytes 4194304 | tf_op jit(solution)/shard_map/all_to_all | solution.py:382
  56.3 0.7 dynamic_slice.6.owner_ref
  56.9 1.3 dynamic_slice.7.blocks_ref
  58.2 4.1 %copy.27 = bf16[384,8,4,128]{3,1,2,0:T(8,128)(2,1)} copy(bf16[384,8,4,128]{3,2,1,0:T(4,128)(2,1)} %bitcast.21) | data formatting | bytes 6291456
  62.5 4.3 %copy.26 = bf16[384,8,4,128]{3,1,2,0:T(8,128)(2,1)} copy(bf16[384,8,4,128]{3,2,1,0:T(4,128)(2,1)} %bitcast.22) | data formatting | bytes 6291456
  66.9 0.7 pad_maximum_fusion.rows_ref
  67.6 2.2 copy_bitcast_fusion.2
  69.8 21.7 %prepare.2 = (bf16[24,2,256,128]{3,2,1,0:T(8,128)(2,1)}, bf16[24,2,256,128]{3,2,1,0:T(8,128)(2,1)}) custom-call(s32[24]{0:T(128)} %dynamic_slice.7.blocks_ref, bf16[3072,256]{1,0:T(8,128)(2,1)} %get-tuple-element.19.q_ref, bf16[3072,256]{1,0:T(8,128)(2,1)} %get-tuple-element.18.k_ref, bf16[3072,512]{1,0:T(8,128)(2,1)} %bitcast.23, ...), custom_call_target="tpu_custom_call" | custom-call | flops 4831838208 | bytes 25165824 | tf_op jit(solution)/shard_map/prepare/pallas_call | solution.py:204
  91.5 9.4 %advance.2 = (bf16[3072,256]{1,0:T(8,128)(2,1)}, bf16[32,2,128,128]{3,2,1,0:T(8,128)(2,1)}) custom-call(s32[24]{0:T(128)} %dynamic_slice.6.owner_ref, s32[24]{0:T(128)} %dynamic_slice.7.blocks_ref, bf16[32,2,128,128]{3,2,1,0:T(8,128)(2,1)} %copy-done.1, bf16[24,2,256,128]{3,2,1,0:T(8,128)(2,1)} %get-tuple-element.10.maps_ref, ...), custom_call_target="tpu_custom_call" | custom-call | flops 402653184 | bytes 16777216 | tf_op jit(solution)/shard_map/advance/pallas_call | solution.py:254
  100.9 4.4 %all-to-all-start.1 = ((bf16[4,768,256]{2,1,0:T(8,128)(2,1)}), bf16[4,768,256]{2,1,0:T(8,128)(2,1)}, u32[]{:S(2)}, u32[]{:S(2)}) async-start(bf16[4,768,256]{2,1,0:T(8,128)(2,1)} %bitcast.25), calls=%async_computation.1 | async-start | bytes 3145728 | tf_op jit(solution)/shard_map/all_to_all | solution.py:416
  105.2 21.6 %prepare.3 = (bf16[24,2,256,128]{3,2,1,0:T(8,128)(2,1)}, bf16[24,2,256,128]{3,2,1,0:T(8,128)(2,1)}) custom-call(s32[24]{0:T(128)} %dynamic_slice.7.blocks_ref, bf16[3072,256]{1,0:T(8,128)(2,1)} %get-tuple-element.19.q_ref, bf16[3072,256]{1,0:T(8,128)(2,1)} %get-tuple-element.18.k_ref, bf16[3072,512]{1,0:T(8,128)(2,1)} %bitcast.24, ...), custom_call_target="tpu_custom_call" | custom-call | flops 4831838208 | bytes 25165824 | tf_op jit(solution)/shard_map/prepare/pallas_call | solution.py:204
  126.9 9.4 %advance.3 = (bf16[3072,256]{1,0:T(8,128)(2,1)}, bf16[32,2,128,128]{3,2,1,0:T(8,128)(2,1)}) custom-call(s32[24]{0:T(128)} %dynamic_slice.6.owner_ref, s32[24]{0:T(128)} %dynamic_slice.7.blocks_ref, bf16[32,2,128,128]{3,2,1,0:T(8,128)(2,1)} %copy-done, bf16[24,2,256,128]{3,2,1,0:T(8,128)(2,1)} %get-tuple-element.13.maps_ref, ...), custom_call_target="tpu_custom_call" | custom-call | flops 402653184 | bytes 16777216 | tf_op jit(solution)/shard_map/advance/pallas_call | solution.py:254
  136.3 36.2 %all_to_all.30.arrived_ref = bf16[32,2,128,128]{3,2,1,0:T(8,128)(2,1)} all-to-all(bf16[32,2,128,128]{3,2,1,0:T(8,128)(2,1)} %get-tuple-element.16), channel_id=1, replica_groups=mesh['req'=32,'head'=4] {'req'}, dimensions={0} | all-to-all | bytes 4194304 | tf_op jit(solution)/shard_map/all_to_all | solution.py:414
  172.5 32.3 %all_to_all.31.arrived_ref = bf16[32,2,128,128]{3,2,1,0:T(8,128)(2,1)} all-to-all(bf16[32,2,128,128]{3,2,1,0:T(8,128)(2,1)S(1)} %copy-done.2), channel_id=1, replica_groups=mesh['req'=32,'head'=4] {'req'}, dimensions={0} | all-to-all | bytes 4194304 | tf_op jit(solution)/shard_map/all_to_all | solution.py:414
  204.8 4.9 %all-to-all-start.3 = ((bf16[4,768,256]{2,1,0:T(8,128)(2,1)}), bf16[4,768,256]{2,1,0:T(8,128)(2,1)S(1)}, u32[]{:S(2)}, u32[]{:S(2)}) async-start(bf16[4,768,256]{2,1,0:T(8,128)(2,1)} %bitcast.4), calls=%async_computation.3 | async-start | bytes 3145728 | tf_op jit(solution)/shard_map/all_to_all | solution.py:416
  209.6 0.1 copy.16
  209.7 0.1 eq.31
  209.9 1.1 select_reduce_fusion.source_ref
  211.0 4.9 %place.2.refs_0_ = f32[24,4,128,128]{3,2,1,0:T(8,128)} custom-call(s32[24]{0:T(128)} %select_reduce_fusion.source_ref, bf16[32,2,128,128]{3,2,1,0:T(8,128)(2,1)} %all_to_all.31.arrived_ref), custom_call_target="tpu_custom_call" | custom-call | bytes 5242880 | tf_op jit(solution)/shard_map/place/pallas_call | solution.py:301
  215.9 4.9 %place.3 = f32[24,4,128,128]{3,2,1,0:T(8,128)} custom-call(s32[24]{0:T(128)} %select_reduce_fusion.source_ref, bf16[32,2,128,128]{3,2,1,0:T(8,128)(2,1)} %all_to_all.30.arrived_ref, f32[24,4,128,128]{3,2,1,0:T(8,128)} %place.2.refs_0_), custom_call_target="tpu_custom_call", output_to_operand_aliasing={{}: (2, {})} | custom-call | bytes 5242880 | tf_op jit(solution)/shard_map/place/pallas_call | solution.py:301
  220.8 9.8 %all-to-all-done.3.refs_1_ = bf16[4,768,256]{2,1,0:T(8,128)(2,1)S(1)} async-done(((bf16[4,768,256]{2,1,0:T(8,128)(2,1)}), bf16[4,768,256]{2,1,0:T(8,128)(2,1)S(1)}, u32[]{:S(2)}, u32[]{:S(2)}) %all-to-all-start.3) | async-done | bytes 1572896 | tf_op jit(solution)/shard_map/all_to_all | solution.py:416
  230.6 1.2 copy-done.3
  231.9 12.3 %project.1 = bf16[768,2048]{1,0:T(8,128)(2,1)} custom-call(bf16[4,768,256]{2,1,0:T(8,128)(2,1)} %all-to-all-done.1.refs_0_, bf16[4,768,256]{2,1,0:T(8,128)(2,1)} %copy-done.3, bf16[2048,2048]{1,0:T(8,128)(2,1)} %all-gather.2.cloned.1.call-done.refs_2_), custom_call_target="tpu_custom_call" | custom-call | flops 6442450944 | bytes 16777216 | tf_op jit(solution)/shard_map/project/pallas_call | solution.py:336
  (28 shorter events, 0.2 us)
Async XLA Ops:
  7.2 0.8 copy-start.10
  7.2 0.9 copy-start.8
  7.2 223.5 %all-gather.2.cloned.1.call-start = ((), (), s32[]{:S(2)}) async-start(), calls=%async_computation.6 | async-start | bytes 10485760 | tf_op jit(solution)/shard_map/all_gather | solution.py:384
  12.5 38.4 %all-to-all-start = ((bf16[32,2,128,128]{3,2,1,0:T(8,128)(2,1)}), bf16[32,2,128,128]{3,2,1,0:T(8,128)(2,1)S(1)}, u32[]{:S(2)}, u32[]{:S(2)}) async-start(bf16[32,2,128,128]{3,2,1,0:T(8,128)(2,1)} %pick_states.2), calls=%async_computation | async-start | bytes 4194304 | tf_op jit(solution)/shard_map/all_to_all | solution.py:382
  51.0 1.3 copy-start.1
  52.3 48.6 %all-to-all-start.2 = ((bf16[32,2,128,128]{3,2,1,0:T(8,128)(2,1)}), bf16[32,2,128,128]{3,2,1,0:T(8,128)(2,1)S(1)}, u32[]{:S(2)}, u32[]{:S(2)}) async-start(bf16[32,2,128,128]{3,2,1,0:T(8,128)(2,1)} %pick_states.3), calls=%async_computation.2 | async-start | bytes 4194304 | tf_op jit(solution)/shard_map/all_to_all | solution.py:382
  58.2 4.2 %copy-start.6 = (f32[3072,4]{0,1:T(4,128)S(1)}, f32[3072,4]{0,1:T(4,128)}, u32[]{:S(2)}) copy-start(f32[3072,4]{0,1:T(4,128)} %param.18) | copy-start | bytes 147460
  58.2 4.2 %copy-start.7 = (f32[3072,4]{0,1:T(4,128)S(1)}, f32[3072,4]{0,1:T(4,128)}, u32[]{:S(2)}) copy-start(f32[3072,4]{0,1:T(4,128)} %param.17) | copy-start | bytes 147460
  62.5 5.1 %copy-start.4 = (bf16[3072,2,128]{2,1,0:T(2,128)(2,1)S(1)}, bf16[3072,2,128]{2,1,0:T(2,128)(2,1)}, u32[]{:S(2)}) copy-start(bf16[3072,2,128]{2,1,0:T(2,128)(2,1)} %param.14) | copy-start | bytes 4718596
  62.5 5.0 %copy-start.5 = (bf16[3072,2,128]{2,1,0:T(2,128)(2,1)S(1)}, bf16[3072,2,128]{2,1,0:T(2,128)(2,1)}, u32[]{:S(2)}) copy-start(bf16[3072,2,128]{2,1,0:T(2,128)(2,1)} %param.13) | copy-start | bytes 4718596
  100.9 26.0 %copy-start = (bf16[32,2,128,128]{3,2,1,0:T(8,128)(2,1)}, bf16[32,2,128,128]{3,2,1,0:T(8,128)(2,1)S(1)}, u32[]{:S(2)}) copy-start(bf16[32,2,128,128]{3,2,1,0:T(8,128)(2,1)S(1)} %all-to-all-done.2.state_ref) | copy-start | bytes 6291460
  100.9 35.4 %all-to-all-start.1 = ((bf16[4,768,256]{2,1,0:T(8,128)(2,1)}), bf16[4,768,256]{2,1,0:T(8,128)(2,1)}, u32[]{:S(2)}, u32[]{:S(2)}) async-start(bf16[4,768,256]{2,1,0:T(8,128)(2,1)} %bitcast.25), calls=%async_computation.1 | async-start | bytes 3145728 | tf_op jit(solution)/shard_map/all_to_all | solution.py:416
  136.3 36.2 %copy-start.2 = (bf16[32,2,128,128]{3,2,1,0:T(8,128)(2,1)S(1)}, bf16[32,2,128,128]{3,2,1,0:T(8,128)(2,1)}, u32[]{:S(2)}) copy-start(bf16[32,2,128,128]{3,2,1,0:T(8,128)(2,1)} %get-tuple-element.17) | copy-start | bytes 6291460
  204.8 5.0 %copy-start.9 = (s32[768]{0:T(1024)S(1)}, s32[768]{0:T(1024)}, u32[]{:S(2)}) copy-start(s32[768]{0:T(1024)} %param.25) | copy-start | bytes 9220
  204.8 25.9 %all-to-all-start.3 = ((bf16[4,768,256]{2,1,0:T(8,128)(2,1)}), bf16[4,768,256]{2,1,0:T(8,128)(2,1)S(1)}, u32[]{:S(2)}, u32[]{:S(2)}) async-start(bf16[4,768,256]{2,1,0:T(8,128)(2,1)} %bitcast.4), calls=%async_computation.3 | async-start | bytes 3145728 | tf_op jit(solution)/shard_map/all_to_all | solution.py:416
  230.6 1.2 copy-start.3
Sparse Core Ops, SparseCore 0:
  9.7 85.5 all-gather.1

commit v2 on v1

v2 whole, which is shorter than its diff:
```python
import functools

import jax
import jax.numpy as jnp
from jax import lax
from jax.experimental import pallas as pl
from jax.experimental.pallas import tpu as pltpu
from jax.sharding import PartitionSpec as P

BLOCK = 64
TAIL_POSITIONS = 128
WIDTH = 128
BASE = 8
EPSILON = 1e-06
HIGHEST = lax.Precision.HIGHEST
BF16 = jnp.bfloat16
F32 = jnp.float32


def iota(shape, dim):
    return lax.broadcasted_iota(jnp.int32, shape, dim)


def dot(left, right, dims=((1,), (0,))):
    return lax.dot_general(left, right, (dims, ((), ())), preferred_element_type=F32)


def params():
    return pltpu.CompilerParams(vmem_limit_bytes=(64 << 20) - (1 << 18))


def pick_kernel(wanted_ref, cache_ref, out_ref, wide, short, in_sems, out_sems):
    slots, count = cache_ref.shape[0], out_ref.shape[0]
    loads = [
        pltpu.make_async_copy(cache_ref.at[i], wide.at[i], in_sems.at[i]) for i in range(slots)
    ]
    for load in loads:
        load.start()
    for i, load in enumerate(loads):
        load.wait()
        short[i] = wide[i].astype(BF16)
    stores = [
        pltpu.make_async_copy(short.at[wanted_ref[i]], out_ref.at[i], out_sems.at[i])
        for i in range(count)
    ]
    for store in stores:
        store.start()
    for store in stores:
        store.wait()


def pick_states(wanted, cache_states):
    count = wanted.shape[0]
    one = cache_states.shape[1:]
    return pl.pallas_call(
        pick_kernel,
        out_shape=jax.ShapeDtypeStruct((count,) + one, BF16),
        grid_spec=pltpu.PrefetchScalarGridSpec(
            num_scalar_prefetch=1,
            grid=(1,),
            in_specs=[pl.BlockSpec(memory_space=pl.ANY)],
            out_specs=pl.BlockSpec(memory_space=pl.ANY),
            scratch_shapes=[
                pltpu.VMEM(cache_states.shape, F32),
                pltpu.VMEM(cache_states.shape, BF16),
                pltpu.SemaphoreType.DMA((cache_states.shape[0],)),
                pltpu.SemaphoreType.DMA((count,)),
            ],
        ),
        compiler_params=params(),
        cost_estimate=pl.CostEstimate(flops=0, bytes_accessed=6 << 20, transcendentals=0),
        name="pick_states",
    )(wanted, cache_states)


def unit_rows(vectors):
    vectors = vectors.astype(F32)
    return vectors * lax.rsqrt(
        jnp.sum(vectors * vectors, axis=-1, keepdims=True) + EPSILON
    )


def unit_lower_inverse(systems):
    count = len(systems)
    shape = (TAIL_POSITIONS, TAIL_POSITIONS)
    row, col = iota(shape, 0), iota(shape, 1)
    parts = TAIL_POSITIONS // BASE
    diagonal = (row // BASE) == (col // BASE)
    packed = []
    for system in systems:
        inner = jnp.where(diagonal, system, 0.0)
        total = inner[:BASE]
        for part in range(1, parts):
            total = total + inner[part * BASE : (part + 1) * BASE]
        packed.append(total)
    short = (BASE, TAIL_POSITIONS)
    lane = iota(short, 1)
    first = jnp.where(iota(short, 0) == lane % BASE, 1.0, 0.0)
    solved = [first] * count
    for step in range(BASE - 1):
        index = (lane // BASE) * BASE + step
        for i in range(count):
            factor = jnp.take_along_axis(packed[i], index, axis=1)
            solved[i] = solved[i] - factor * solved[i][step : step + 1]
    inverses = [
        jnp.where(diagonal, jnp.concatenate([x] * parts, axis=0), 0.0) for x in solved
    ]
    size = BASE
    while size < TAIL_POSITIONS:
        if size * 2 < TAIL_POSITIONS:
            below = ((row // (2 * size)) == (col // (2 * size))) & (
                (row // size) != (col // size)
            )
            short_inv = [x.astype(BF16) for x in inverses]
            moved = [
                dot(jnp.where(below, system, 0.0).astype(BF16), x).astype(BF16)
                for system, x in zip(systems, short_inv)
            ]
            inverses = [
                x - dot(s, m) for x, s, m in zip(inverses, short_inv, moved)
            ]
        else:
            short_inv = [x.astype(BF16) for x in inverses]
            moved = [
                dot(system[size:, :size].astype(BF16), x[:size, :size]).astype(BF16)
                for system, x in zip(systems, short_inv)
            ]
            corner = [dot(x[size:, size:], m) for x, m in zip(short_inv, moved)]
            inverses = [
                jnp.concatenate(
                    [x[:size], jnp.concatenate([-c, x[size:, size:]], axis=1)], axis=0
                )
                for x, c in zip(inverses, corner)
            ]
        size *= 2
    return inverses


def prep_kernel(per_step, blocks_ref, q_ref, k_ref, v_ref, rows_ref, core_ref, final_ref):
    step = pl.program_id(0)
    tokens = TAIL_POSITIONS
    square = (tokens, tokens)
    row, col = iota(square, 0), iota(square, 1)
    upto = jnp.where(row <= col, 1.0, 0.0)
    within = row >= col
    strict = row > col
    scale = WIDTH ** (-0.5)

    masked = []
    for r in range(per_step):
        live = iota((4, tokens), 1) < blocks_ref[step * per_step + r] * BLOCK
        masked.append(jnp.where(live, rows_ref[0, :, r * tokens : (r + 1) * tokens], 0.0))
    masked = jnp.concatenate(masked, axis=0)
    running = lax.dot_general(
        masked, upto, (((1,), (0,)), ((), ())), precision=HIGHEST, preferred_element_type=F32
    )
    tall = jnp.transpose(jnp.concatenate([masked, running], axis=0))

    keys, queries, systems, fades, scores = [], [], [], [], []
    for r in range(per_step):
        span = pl.ds(r * tokens, tokens)
        k = unit_rows(k_ref[span, :]).astype(BF16)
        q = (unit_rows(q_ref[span, :]) * scale).astype(BF16)
        keys.append(k)
        queries.append(q)
        pair = dot(jnp.concatenate([k, q], axis=0), k, ((1,), (1,)))
        for h in range(2):
            at = r * 4 + 2 + h
            run_row = running[at : at + 1]
            run_col = tall[:, per_step * 4 + at : per_step * 4 + at + 1]
            rate_col = tall[:, r * 4 + h : r * 4 + h + 1]
            fade = jnp.exp(jnp.where(within, run_col - run_row, -1e30))
            systems.append(jnp.where(strict, rate_col * pair[:tokens] * fade, 0.0))
            scores.append((pair[tokens:] * fade).astype(BF16))
    inverses = unit_lower_inverse(systems)
    solved = []
    for r in range(per_step):
        key_wide = keys[r].astype(F32)
        for h in range(2):
            i = r * 2 + h
            at = r * 4 + 2 + h
            grow_col = jnp.exp(tall[:, per_step * 4 + at : per_step * 4 + at + 1])
            rate_row = masked[r * 4 + h : r * 4 + h + 1]
            left = (inverses[i] * rate_row).astype(BF16)
            right = jnp.concatenate(
                [
                    v_ref[pl.ds(r * tokens, tokens), h * WIDTH : (h + 1) * WIDTH],
                    (key_wide * grow_col).astype(BF16),
                ],
                axis=1,
            )
            solved.append(dot(left, right).astype(BF16))
    for r in range(per_step):
        key_turned = jnp.transpose(keys[r].astype(F32))
        query_wide = queries[r].astype(F32)
        for h in range(2):
            i = r * 2 + h
            at = r * 4 + 2 + h
            run_row = running[at : at + 1]
            end = run_row[:, tokens - 1 : tokens]
            grow_col = jnp.exp(tall[:, per_step * 4 + at : per_step * 4 + at + 1])
            ending = (key_turned * jnp.exp(end - run_row)).astype(BF16)
            both = dot(jnp.concatenate([scores[i], ending], axis=0), solved[i])
            kept = jnp.where(row == col, jnp.exp(end), 0.0)
            core_ref[r, h, :WIDTH] = (query_wide * grow_col - both[:tokens, WIDTH:]).astype(BF16)
            core_ref[r, h, WIDTH:] = both[:tokens, :WIDTH].astype(BF16)
            final_ref[r, h, :WIDTH] = (kept - both[tokens:, WIDTH:]).astype(BF16)
            final_ref[r, h, WIDTH:] = both[tokens:, :WIDTH].astype(BF16)


def prepare(blocks, queries, keys, values, rows):
    requests = blocks.shape[0]
    chunks = rows.shape[0]
    per_step = 8 if requests % 8 == 0 else 4
    span = per_step * TAIL_POSITIONS
    tall = (requests, 2 * chunks, 2 * WIDTH, WIDTH)
    block = pl.BlockSpec((per_step, 2) + tall[2:], lambda s, c, _: (s, c, 0, 0))
    return pl.pallas_call(
        functools.partial(prep_kernel, per_step),
        out_shape=(jax.ShapeDtypeStruct(tall, BF16), jax.ShapeDtypeStruct(tall, BF16)),
        grid_spec=pltpu.PrefetchScalarGridSpec(
            num_scalar_prefetch=1,
            grid=(requests // per_step, chunks),
            in_specs=[
                pl.BlockSpec((span, WIDTH), lambda s, c, _: (s, c)),
                pl.BlockSpec((span, WIDTH), lambda s, c, _: (s, c)),
                pl.BlockSpec((span, 2 * WIDTH), lambda s, c, _: (s, c)),
                pl.BlockSpec((1, 4, span), lambda s, c, _: (c, 0, s)),
            ],
            out_specs=(block, block),
        ),
        compiler_params=params(),
        cost_estimate=pl.CostEstimate(
            flops=requests * 4 * 24 * 2 * 128**3, bytes_accessed=24 << 20, transcendentals=0
        ),
        name="prepare",
    )(blocks, queries, keys, values, rows)


def finish_kernel(owner_ref, state_ref, maps_ref, out_ref, states, maps, finals, state_sems, map_sems, out_sems):
    requests, heads = maps_ref.shape[:2]
    loads = []
    for r in range(requests):
        pair = (
            pltpu.make_async_copy(state_ref.at[owner_ref[r]], states.at[r], state_sems.at[r]),
            pltpu.make_async_copy(maps_ref.at[r], maps.at[r], map_sems.at[r]),
        )
        for load in pair:
            load.start()
        loads.append(pair)
    stores = []
    for r in range(requests):
        for load in loads[r]:
            load.wait()
        for h in range(heads):
            moved = dot(maps[r, h, :WIDTH], states[r, h])
            finals[r, h] = (moved + maps[r, h, WIDTH:].astype(F32)).astype(BF16)
        store = pltpu.make_async_copy(finals.at[r], out_ref.at[owner_ref[r]], out_sems.at[r])
        store.start()
        stores.append(store)
    for store in stores:
        store.wait()


def finish(owners, states, maps):
    requests = maps.shape[0]
    one = states.shape[1:]
    return pl.pallas_call(
        finish_kernel,
        out_shape=jax.ShapeDtypeStruct(states.shape, BF16),
        grid_spec=pltpu.PrefetchScalarGridSpec(
            num_scalar_prefetch=1,
            grid=(1,),
            in_specs=[pl.BlockSpec(memory_space=pl.ANY)] * 2,
            out_specs=pl.BlockSpec(memory_space=pl.ANY),
            scratch_shapes=[
                pltpu.VMEM((requests,) + one, BF16),
                pltpu.VMEM(maps.shape, BF16),
                pltpu.VMEM((requests,) + one, BF16),
                pltpu.SemaphoreType.DMA((requests,)),
                pltpu.SemaphoreType.DMA((requests,)),
                pltpu.SemaphoreType.DMA((requests,)),
            ],
        ),
        compiler_params=params(),
        cost_estimate=pl.CostEstimate(
            flops=requests * 4 * 2 * 128**3, bytes_accessed=13 << 20, transcendentals=0
        ),
        name="finish",
    )(owners, states, maps)


def block_at(step, group_ref, group_steps, groups, shifts):
    shift = shifts[-1]
    for i in range(len(shifts) - 1):
        shift = jnp.where(step // group_steps == i, shifts[i], shift)
    return ((group_ref[0] + shift) % groups) * group_steps + step % group_steps


def emit_kernel(per_step, group_steps, groups, shifts, owner_ref, blocks_ref, group_ref, *refs):
    state_refs = refs[:per_step]
    maps_ref, gate_ref, gain_ref = refs[per_step : per_step + 3]
    out_refs = refs[per_step + 3 :]
    step = pl.program_id(0)
    first = block_at(step, group_ref, group_steps, groups, shifts) * per_step
    tokens = TAIL_POSITIONS
    heads = maps_ref.shape[1]
    gain = gain_ref[...]
    rows = []
    for r in range(per_step):
        live = iota((tokens, WIDTH), 0) < blocks_ref[first + r] * BLOCK
        parts = []
        for h in range(heads):
            core = dot(maps_ref[r, h, :WIDTH], state_refs[r][0, h]) + maps_ref[r, h, WIDTH:].astype(F32)
            gate = gate_ref[pl.ds(r * tokens, tokens), h * WIDTH : (h + 1) * WIDTH].astype(F32)
            spread = jnp.mean(core * core, axis=-1, keepdims=True)
            normed = core * lax.rsqrt(spread + EPSILON) * gain * (gate / (1.0 + jnp.exp(-gate)))
            parts.append(jnp.where(live, normed, 0.0).astype(BF16))
        rows.append(jnp.concatenate(parts, axis=1))
    for i in range(len(shifts)):

        @pl.when(step // group_steps == i)
        def _(i=i):
            for r in range(per_step):
                out_refs[i][pl.ds(r * tokens, tokens), :] = rows[r]


def emit(owners, blocks, group, groups, shifts, states, maps, gates, gain):
    requests = blocks.shape[0]
    share = requests // groups
    per_step = 6 if share % 6 == 0 else 1
    group_steps = share // per_step
    span = per_step * TAIL_POSITIONS
    heads = maps.shape[1]

    def at(step, group_ref):
        return block_at(step, group_ref, group_steps, groups, shifts)

    def state_spec(r):
        return pl.BlockSpec(
            (1,) + states.shape[1:], lambda s, o, b, g: (o[at(s, g) * per_step + r], 0, 0, 0)
        )

    def out_spec(i):
        return pl.BlockSpec(
            (span, heads * WIDTH),
            lambda s, o, b, g: (jnp.clip(s - i * group_steps, 0, group_steps - 1), 0),
        )

    return pl.pallas_call(
        functools.partial(emit_kernel, per_step, group_steps, groups, shifts),
        out_shape=[
            jax.ShapeDtypeStruct((share * TAIL_POSITIONS, heads * WIDTH), BF16)
            for _ in shifts
        ],
        grid_spec=pltpu.PrefetchScalarGridSpec(
            num_scalar_prefetch=3,
            grid=(len(shifts) * group_steps,),
            in_specs=[state_spec(r) for r in range(per_step)]
            + [
                pl.BlockSpec((per_step,) + maps.shape[1:], lambda s, o, b, g: (at(s, g), 0, 0, 0)),
                pl.BlockSpec((span, heads * WIDTH), lambda s, o, b, g: (at(s, g), 0)),
                pl.BlockSpec((1, WIDTH), lambda s, o, b, g: (0, 0)),
            ],
            out_specs=[out_spec(i) for i in range(len(shifts))],
        ),
        compiler_params=params(),
        cost_estimate=pl.CostEstimate(
            flops=requests * 4 * 2 * 128**3, bytes_accessed=16 << 20, transcendentals=0
        ),
        name="emit",
    )(owners, blocks, group, *([states] * per_step), maps, gates, gain)


def place_kernel(source_ref, arrived_ref, out_ref, short, wide, in_sems, out_sems):
    slots = out_ref.shape[0]
    loads = [
        pltpu.make_async_copy(arrived_ref.at[source_ref[i]], short.at[i], in_sems.at[i])
        for i in range(slots)
    ]
    for load in loads:
        load.start()
    stores = []
    for i in range(slots):
        loads[i].wait()
        wide[i] = short[i].astype(F32)
        store = pltpu.make_async_copy(wide.at[i], out_ref.at[i], out_sems.at[i])
        store.start()
        stores.append(store)
    for store in stores:
        store.wait()


def place(source, arrived):
    slots = source.shape[0]
    shape = (slots,) + arrived.shape[1:]
    return pl.pallas_call(
        place_kernel,
        out_shape=jax.ShapeDtypeStruct(shape, F32),
        grid_spec=pltpu.PrefetchScalarGridSpec(
            num_scalar_prefetch=1,
            grid=(1,),
            in_specs=[pl.BlockSpec(memory_space=pl.ANY)],
            out_specs=pl.BlockSpec(memory_space=pl.ANY),
            scratch_shapes=[
                pltpu.VMEM(shape, BF16),
                pltpu.VMEM(shape, F32),
                pltpu.SemaphoreType.DMA((slots,)),
                pltpu.SemaphoreType.DMA((slots,)),
            ],
        ),
        compiler_params=params(),
        cost_estimate=pl.CostEstimate(flops=0, bytes_accessed=10 << 20, transcendentals=0),
        name="place",
    )(source, arrived)


def project_kernel(count, half, place_ref, *refs):
    shares, nears, fars = (refs[i * count : (i + 1) * count] for i in range(3))
    out_ref = refs[-1]
    total = refs[-2][...].astype(F32) if len(refs) > 1 + 3 * count else None
    near_at = pl.multiple_of(place_ref[0] * half, half)
    far_at = pl.multiple_of((1 - place_ref[0]) * half, half)
    for share, near, far in zip(shares, nears, fars):
        for weight, at in ((near, near_at), (far, far_at)):
            term = dot(share[:, pl.ds(at, half)], weight[...])
            total = term if total is None else total + term
    out_ref[...] = total.astype(BF16)


def project(core, shares, nears, fars, earlier):
    rows, width = shares[0].shape
    half = width // 2
    model = nears[0].shape[1]
    tile = min(512, model)

    def weight_spec(weight, far):
        if weight.shape[0] == half:
            return pl.BlockSpec((half, tile), lambda n, _: (0, n))
        return pl.BlockSpec((half, tile), lambda n, c: ((1 - c[0]) if far else c[0], n))

    out_spec = pl.BlockSpec((rows, tile), lambda n, _: (0, n))
    more = [] if earlier is None else [earlier]
    return pl.pallas_call(
        functools.partial(project_kernel, len(shares), half),
        out_shape=jax.ShapeDtypeStruct((rows, model), BF16),
        grid_spec=pltpu.PrefetchScalarGridSpec(
            num_scalar_prefetch=1,
            grid=(model // tile,),
            in_specs=[pl.BlockSpec(a.shape, lambda n, _: (0, 0)) for a in shares]
            + [weight_spec(w, False) for w in nears]
            + [weight_spec(w, True) for w in fars]
            + [out_spec] * len(more),
            out_specs=out_spec,
        ),
        compiler_params=params(),
        cost_estimate=pl.CostEstimate(
            flops=4 * rows * len(shares) * half * model, bytes_accessed=12 << 20, transcendentals=0
        ),
        name="project",
    )(core, *shares, *nears, *fars, *more)


def local(
    queries,
    key_rows,
    values,
    gate_input,
    write_rate,
    log_decay,
    norm_gain,
    out_weight,
    cache_states,
    cache_owner,
    cache_slot,
    suffix_blocks,
    new_slot,
):
    owner_count = lax.axis_size("req")
    groups = lax.axis_size("head")
    device = lax.axis_index("req")
    tokens = queries.shape[0]
    requests = tokens // TAIL_POSITIONS
    heads_all = values.shape[1]
    chunks = queries.shape[1]
    heads = heads_all // chunks

    naming = cache_owner.reshape(owner_count, requests) == device
    wanted = jnp.sum(jnp.where(naming, cache_slot.reshape(owner_count, requests), 0), axis=1)
    picked = pick_states(wanted, cache_states)
    arrived = lax.all_to_all(picked, "req", split_axis=0, concat_axis=0, tiled=True)

    my_owner = lax.dynamic_slice_in_dim(cache_owner, device * requests, requests)
    my_blocks = lax.dynamic_slice_in_dim(suffix_blocks, device * requests, requests)
    slot_ids = jnp.arange(requests, dtype=jnp.int32)
    claimed = naming[None] & (
        new_slot.reshape(owner_count, requests)[None] == slot_ids[:, None, None]
    )
    device_ids = jnp.arange(owner_count, dtype=jnp.int32)[None, :, None]
    source = jnp.sum(jnp.where(claimed, device_ids, 0), axis=(1, 2))

    query_flat = queries.reshape(tokens, -1)
    key_flat = key_rows.reshape(tokens, -1)
    value_flat = values.reshape(tokens, -1)
    gate_flat = gate_input.reshape(tokens, -1)
    half = out_weight.shape[0] // 2
    core = device % 2
    out_weight, key_flat = lax.optimization_barrier((out_weight, key_flat))
    own_rows = lax.dynamic_slice_in_dim(out_weight, core * half, half)
    nears = [
        lax.ppermute(own_rows, "head", [(i, (i + d) % groups) for i in range(groups)])
        for d in range(1, groups)
    ]
    rows = jnp.concatenate(
        [
            write_rate.T.reshape(chunks, heads, tokens),
            log_decay.T.reshape(chunks, heads, tokens),
        ],
        axis=1,
    )
    gain = norm_gain.reshape(1, -1)

    core_maps, final_maps = prepare(my_blocks, query_flat, key_flat, value_flat, rows)
    gate_flat, my_owner, nears, arrived, final_maps = lax.optimization_barrier(
        (gate_flat, my_owner, nears, arrived, final_maps)
    )
    swap = [(i, i ^ 1) for i in range(owner_count)]
    fars = [lax.ppermute(w, "req", swap) for w in nears]
    final = finish(my_owner, arrived, final_maps)
    fars, final = lax.optimization_barrier((fars, final))
    returned = lax.all_to_all(final, "req", split_axis=0, concat_axis=0, tiled=True)
    group = lax.axis_index("head")
    shares = [None] * groups
    order = sorted(range(groups), key=lambda d: -min(d, groups - d))
    for shifts in (order[:1], order[1:]):
        made = emit(
            my_owner, my_blocks, group.reshape(1), groups, shifts, arrived, core_maps, gate_flat, gain
        )
        for d, share in zip(shifts, made):
            pairs = [(i, (i + d) % groups) for i in range(groups)]
            shares[d] = lax.ppermute(share, "head", pairs) if d else share
    early, late = order[:1] + order[-1:], order[1:-1]
    layer_out = None
    for shifts in (early, late):
        if shifts:
            weights = [[[out_weight, *part][d] for d in shifts] for part in (nears, fars)]
            taken = [[shares[d] for d in shifts], *weights]
            layer_out = project(core.reshape(1), *taken, layer_out)
    returned, layer_out = lax.optimization_barrier((returned, layer_out))
    new_cache = place(source, returned)
    return (layer_out, new_cache)


def solution(mesh):
    return jax.shard_map(
        local,
        mesh=mesh,
        in_specs=(
            P("req", "head", None),
            P("req", "head", None),
            P("req", "head", None),
            P("req", "head", None),
            P("req", "head"),
            P("req", "head"),
            P(),
            P("head", None),
            P("req", "head", None, None),
            P(),
            P(),
            P(),
            P(),
        ),
        out_specs=(P(("req", "head"), None), P("req", "head", None, None)),
        check_vma=False,
    )
```

time: 252 us -> 146 us (0.58)
  blocking collectives: 68.4 us -> 0 us
  Pallas kernels: 92 us -> 73.5 us
  between operations: 14.2 us -> 0.96 us
  waiting for transfers between devices: 36.5 us -> 23.5 us
  starting transfers between devices: 21.7 us -> 28.3 us
    all_to_all x2 -> x0, blocking collectives: 68.4 us -> none  [local(): lax.all_to_all(final, 'req', split_axis=0, concat_axis=0, tiled=True)]
    all_to_all x4 -> x2, waiting for transfers between devices: 35.9 us -> 2.61 us  [the longest x1 2.61 us: local(): lax.all_to_all(final, 'req', split_axis=0, concat_axis=0, tiled=True)]
    ppermute x0 -> x9, waiting for transfers between devices: none -> 20.9 us  [the longest x3 15.2 us: local(): shares[d] = lax.ppermute(share, 'head', pairs) if d else share]
    pallas_call x2 -> x1, Pallas kernels: 43.3 us -> 28.8 us  [prepare(): pl.pallas_call(functools.partial(prep_kernel, per_step), out_shape=(jax.S...]
    ppermute x0 -> x9, starting transfers between devices: none -> 12.1 us  [the longest x3 5.88 us: local(): shares[d] = lax.ppermute(share, 'head', pairs) if d else share]
    all_to_all x4 -> x2, starting transfers between devices: 21.7 us -> 16.2 us  [the longest x1 8.56 us: local(): lax.all_to_all(picked, 'req', split_axis=0, concat_axis=0, tiled=True)]
    pallas_call x7, Pallas kernels: 48.7 us -> 44.8 us  [the longest x2 15.2 us: project(): pl.pallas_call(functools.partial(project_kernel, len(shares), half), out_...]
    unnamed x24 -> x16, local copies, waits for them, and re-layouts: 11.1 us -> 9.79 us
  transfers between devices with their start and end apart: 5 -> 11, of which waited for: 2 -> 4; matrix products, arithmetic and copies ran while one was open for 6% -> 11% of each run, Pallas kernels for 32% -> 44%
where the time goes in v2:
time: 146 us; the launch traced here: 145 us
  Pallas kernels  73.5 us (50%)
  starting transfers between devices  28.3 us (19%)
  waiting for transfers between devices  23.5 us (16%)
  local copies, waits for them, and re-layouts  15.9 us (11%)
  other arithmetic  3.03 us (2%)
    pallas_call x1, Pallas kernels, prepare(): pl.pallas_call(functools.partial(prep_kernel, per_step), out_shape=(jax.S...  28.8 us
    ppermute x3, waiting for transfers between devices, local(): shares[d] = lax.ppermute(share, 'head', pairs) if d else share  15.2 us
    pallas_call x2, Pallas kernels, project(): pl.pallas_call(functools.partial(project_kernel, len(shares), half), out_...  15.2 us
    pallas_call x2, Pallas kernels, emit(): pl.pallas_call(functools.partial(emit_kernel, per_step, group_steps, grou...  13.1 us
    unnamed x16, local copies, waits for them, and re-layouts  9.79 us
    all_to_all x1, starting transfers between devices, local(): lax.all_to_all(picked, 'req', split_axis=0, concat_axis=0, tiled=True)  8.56 us
    all_to_all x1, starting transfers between devices, local(): lax.all_to_all(final, 'req', split_axis=0, concat_axis=0, tiled=True)  7.61 us
    pallas_call x1, Pallas kernels, finish(): pl.pallas_call(finish_kernel, out_shape=jax.ShapeDtypeStruct(states.shape...  7.25 us
  transfers between devices with their start and end apart: 11, of which 4 were waited for; matrix products, arithmetic and copies ran while one was open for 11% of the time, Pallas kernels for 44%

profile of v2, /device:TPU:0, one launch (start us, length us, event | category | flops | bytes accessed | tf_op | source)
XLA Modules:
  0.0 145.2 jit_solution(7700124521158687870)
XLA Ops:
  0.6 0.7 broadcast_compare_fusion
  1.4 0.8 reshape.47
  2.2 0.6 select_reduce_fusion.1.wanted_ref
  2.8 4.6 %pick_states.1 = bf16[32,4,128,128]{3,2,1,0:T(8,128)(2,1)} custom-call(s32[32]{0:T(128)} %select_reduce_fusion.1.wanted_ref, f32[8,4,128,128]{3,2,1,0:T(8,128)} %cache_ref.1), custom_call_target="tpu_custom_call" | custom-call | bytes 6291456 | tf_op jit(solution)/shard_map/pick_states/pallas_call | solution.py:55
  7.4 8.6 %all-to-all-start = ((bf16[32,4,128,128]{3,2,1,0:T(8,128)(2,1)}), bf16[32,4,128,128]{3,2,1,0:T(8,128)(2,1)}, u32[]{:S(2)}, u32[]{:S(2)}) async-start(bf16[32,4,128,128]{3,2,1,0:T(8,128)(2,1)} %pick_states.1), calls=%async_computation | async-start | bytes 8388608 | tf_op jit(solution)/shard_map/all_to_all | solution.py:491
  16.0 2.9 %copy.28 = bf16[384,8,2,128]{3,1,2,0:T(8,128)(2,1)} copy(bf16[384,8,2,128]{3,2,1,0:T(2,128)(2,1)} %bitcast.26) | data formatting | bytes 3145728
  19.0 2.3 %constant_dynamic-slice_fusion = bf16[256,2048]{1,0:T(8,128)(2,1)} fusion(bf16[512,2048]{1,0:T(8,128)(2,1)} %refs_5_, s32[]{:T(128)S(6)} %select_n.24), kind=kLoop, calls=%fused_computation.10 | loop fusion | bytes 2097156 | tf_op jit(solution)/shard_map/dynamic_slice | solution.py:509
  21.3 1.5 %collective-permute-start = (bf16[256,2048]{1,0:T(8,128)(2,1)}, bf16[256,2048]{1,0:T(8,128)(2,1)}, u32[]{:S(2)}, u32[]{:S(2)}) collective-permute-start(bf16[256,2048]{1,0:T(8,128)(2,1)} %constant_dynamic-slice_fusion), channel_id=1, source_target_pairs={{0,1},{1,2},{2,3},{3,0},{4,5},{5,6},{6,7},{7,4},{8,9},{9,10},{10,1... | collective-permute-start | bytes 3145736 | tf_op jit(solution)/shard_map/ppermute | solution.py:511
  22.8 2.7 %collective-permute-start.1 = (bf16[256,2048]{1,0:T(8,128)(2,1)}, bf16[256,2048]{1,0:T(8,128)(2,1)}, u32[]{:S(2)}, u32[]{:S(2)}) collective-permute-start(bf16[256,2048]{1,0:T(8,128)(2,1)} %constant_dynamic-slice_fusion), channel_id=1, source_target_pairs={{0,2},{1,3},{2,0},{3,1},{4,6},{5,7},{6,4},{7,5},{8,10},{9,11},{10,... | collective-permute-start | bytes 3145736 | tf_op jit(solution)/shard_map/ppermute | solution.py:511
  25.5 1.4 collective-permute-start.2
  27.1 0.7 pad_maximum_fusion.rows_ref
  27.7 1.3 dynamic_slice.9.owner_ref
  29.0 1.3 dynamic_slice.11.blocks_ref
  30.3 2.2 %copy.25 = bf16[384,8,4,128]{3,1,2,0:T(8,128)(2,1)} copy(bf16[384,8,4,128]{3,2,1,0:T(4,128)(2,1)S(1)} %bitcast.23) | data formatting | bytes 6291456
  32.5 1.4 copy.27
  33.9 1.1 copy-done.1
  35.0 2.2 %copy.26 = bf16[384,8,4,128]{3,1,2,0:T(8,128)(2,1)} copy(bf16[384,8,4,128]{3,2,1,0:T(4,128)(2,1)S(1)} %bitcast.24) | data formatting | bytes 6291456
  37.1 28.8 %prepare.1 = (bf16[24,4,256,128]{3,2,1,0:T(8,128)(2,1)}, bf16[24,4,256,128]{3,2,1,0:T(8,128)(2,1)}) custom-call(s32[24]{0:T(128)} %dynamic_slice.11.blocks_ref, bf16[3072,256]{1,0:T(8,128)(2,1)} %bitcast.29, bf16[3072,256]{1,0:T(8,128)(2,1)} %bitcast.28, bf16[3072,512]{1,0:T(8,128)(2,1)} %bitcast.25, f32[2,4,3072]{2,1,0:T(4,128)} %pad_maximum_fusion.rows_ref), custom_call_target="tpu_custom_call" | custom-call | flops 9663676416 | bytes 25165824 | tf_op jit(solution)/shard_map/prepare/pallas_call | solution.py:218
  65.9 5.6 %collective-permute-done.1.refs_2_ = bf16[256,2048]{1,0:T(8,128)(2,1)} collective-permute-done((bf16[256,2048]{1,0:T(8,128)(2,1)}, bf16[256,2048]{1,0:T(8,128)(2,1)}, u32[]{:S(2)}, u32[]{:S(2)}) %collective-permute-start.1) | collective-permute-done | bytes 1048608 | tf_op jit(solution)/shard_map/ppermute | solution.py:511
  72.2 7.2 %finish.1 = bf16[32,4,128,128]{3,2,1,0:T(8,128)(2,1)} custom-call(s32[24]{0:T(128)} %dynamic_slice.9.owner_ref, bf16[32,4,128,128]{3,2,1,0:T(8,128)(2,1)} %all-to-all-done.state_ref.refs_0_.refs_1_.refs_2_.refs_3_.refs_4_.refs_5_, bf16[24,4,256,128]{3,2,1,0:T(8,128)(2,1)} %get-tuple-element.30.maps_ref), custom_call_target="tpu_custom_call" | custom-call | flops 402653184 | bytes 13631488 | tf_op jit(solution)/shard_map/finish/pallas_call | solution.py:268
  79.4 7.6 %all-to-all-start.1 = ((bf16[32,4,128,128]{3,2,1,0:T(8,128)(2,1)}), bf16[32,4,128,128]{3,2,1,0:T(8,128)(2,1)}, u32[]{:S(2)}, u32[]{:S(2)}) async-start(bf16[32,4,128,128]{3,2,1,0:T(8,128)(2,1)} %finish.1), calls=%async_computation.1 | async-start | bytes 8388608 | tf_op jit(solution)/shard_map/all_to_all | solution.py:531
  87.1 4.6 %emit.3 = bf16[768,512]{1,0:T(8,128)(2,1)} custom-call(s32[24]{0:T(128)} %dynamic_slice.9.owner_ref, s32[24]{0:T(128)} %dynamic_slice.11.blocks_ref, s32[1]{0:T(128)} %bitcast.3.group_ref, bf16[32,4,128,128]{3,2,1,0:T(8,128)(2,1)} %all-to-all-done.state_ref.refs_0_.refs_1_.refs_2_.refs_3_.refs_4_.refs_5_, ...), custom_call_target="tpu_custom_call" | custom-call | flops 402653184 | bytes 16777216 | tf_op jit(solution)/shard_map/emit/pallas_call | solution.py:350
  91.7 2.6 %collective-permute-start.8 = (bf16[768,512]{1,0:T(8,128)(2,1)}, bf16[768,512]{1,0:T(8,128)(2,1)}, u32[]{:S(2)}, u32[]{:S(2)}) collective-permute-start(bf16[768,512]{1,0:T(8,128)(2,1)} %emit.3), channel_id=1, source_target_pairs={{0,2},{1,3},{2,0},{3,1},{4,6},{5,7},{6,4},{7,5},{8,10},{9,11},{10,... | collective-permute-start | bytes 2359304 | tf_op jit(solution)/shard_map/ppermute | solution.py:541
  94.3 8.6 %emit.2 = (bf16[768,512]{1,0:T(8,128)(2,1)}, bf16[768,512]{1,0:T(8,128)(2,1)}, bf16[768,512]{1,0:T(8,128)(2,1)}) custom-call(s32[24]{0:T(128)} %dynamic_slice.9.owner_ref, s32[24]{0:T(128)} %dynamic_slice.11.blocks_ref, s32[1]{0:T(128)} %bitcast.3.group_ref, bf16[32,4,128,128]{3,2,1,0:T(8,128)(2,1)} %all-to-all-done.state_ref.refs_0_.refs_1_.refs_2_.refs_3_.refs_4_.refs_5_, ...), custom_call_target="tpu_custom_call" | custom-call | flops 402653184 | bytes 16777216 | tf_op jit(solution)/shard_map/emit/pallas_call | solution.py:350
  103.3 2.8 %collective-permute-start.7 = (bf16[768,512]{1,0:T(8,128)(2,1)}, bf16[768,512]{1,0:T(8,128)(2,1)}, u32[]{:S(2)}, u32[]{:S(2)}) collective-permute-start(bf16[768,512]{1,0:T(8,128)(2,1)} %get-tuple-element.35), channel_id=1, source_target_pairs={{0,3},{1,0},{2,1},{3,2},{4,7},{5,4},{6,5},{7,6},{8,11},{9,8},{10,9... | collective-permute-start | bytes 2359304 | tf_op jit(solution)/shard_map/ppermute | solution.py:541
  106.3 1.0 select_reduce_fusion.source_ref
  107.4 6.5 %collective-permute-done.8.refs_0_ = bf16[768,512]{1,0:T(8,128)(2,1)} collective-permute-done((bf16[768,512]{1,0:T(8,128)(2,1)}, bf16[768,512]{1,0:T(8,128)(2,1)}, u32[]{:S(2)}, u32[]{:S(2)}) %collective-permute-start.8) | collective-permute-done | bytes 786464 | tf_op jit(solution)/shard_map/ppermute | solution.py:541
  113.9 7.2 %project.2.refs_6_ = bf16[768,2048]{1,0:T(8,128)(2,1)} custom-call(s32[1]{0:T(128)} %bitcast.2.place_ref, bf16[768,512]{1,0:T(8,128)(2,1)} %collective-permute-done.8.refs_0_, bf16[768,512]{1,0:T(8,128)(2,1)} %get-tuple-element.38.refs_1_, bf16[256,2048]{1,0:T(8,128)(2,1)} %collective-permute-done.1.refs_2_, bf16[512,2048]{1,0:T(8,128)(2,1)} %refs_5_, ...), custom_call_target="tpu_custom_call" | custom-call | flops 3221225472 | bytes 12582912 | tf_op jit(solution)/shard_map/project/pallas_call | solution.py:444
  121.2 8.7 %collective-permute-done.6.refs_0_ = bf16[768,512]{1,0:T(8,128)(2,1)} collective-permute-done((bf16[768,512]{1,0:T(8,128)(2,1)}, bf16[768,512]{1,0:T(8,128)(2,1)}, u32[]{:S(2)}, u32[]{:S(2)}) %collective-permute-start.6) | collective-permute-done | bytes 786464 | tf_op jit(solution)/shard_map/ppermute | solution.py:541
  129.8 7.9 %project.3 = bf16[768,2048]{1,0:T(8,128)(2,1)} custom-call(s32[1]{0:T(128)} %bitcast.2.place_ref, bf16[768,512]{1,0:T(8,128)(2,1)} %collective-permute-done.6.refs_0_, bf16[768,512]{1,0:T(8,128)(2,1)} %collective-permute-done.7.refs_1_, bf16[256,2048]{1,0:T(8,128)(2,1)} %collective-permute-done.refs_2_, bf16[256,2048]{1,0:T(8,128)(2,1)} %collective-permute-done.2.refs_3_, ...), custom_call_target="tpu_custom_call" | custom-call | flops 3221225472 | bytes 12582912 | tf_op jit(solution)/shard_map/project/pallas_call | solution.py:444
  137.7 2.6 %all-to-all-done.1.arrived_ref = bf16[32,4,128,128]{3,2,1,0:T(8,128)(2,1)} async-done(((bf16[32,4,128,128]{3,2,1,0:T(8,128)(2,1)}), bf16[32,4,128,128]{3,2,1,0:T(8,128)(2,1)}, u32[]{:S(2)}, u32[]{:S(2)}) %all-to-all-start.1) | async-done | bytes 4194336 | tf_op jit(solution)/shard_map/all_to_all | solution.py:531
  140.4 4.6 %place.1 = f32[24,4,128,128]{3,2,1,0:T(8,128)} custom-call(s32[24]{0:T(128)} %select_reduce_fusion.source_ref, bf16[32,4,128,128]{3,2,1,0:T(8,128)(2,1)} %all-to-all-done.1.arrived_ref), custom_call_target="tpu_custom_call" | custom-call | bytes 10485760 | tf_op jit(solution)/shard_map/place/pallas_call | solution.py:397
  (28 shorter events, 1.5 us)
Async XLA Ops:
  7.4 64.1 %all-to-all-start = ((bf16[32,4,128,128]{3,2,1,0:T(8,128)(2,1)}), bf16[32,4,128,128]{3,2,1,0:T(8,128)(2,1)}, u32[]{:S(2)}, u32[]{:S(2)}) async-start(bf16[32,4,128,128]{3,2,1,0:T(8,128)(2,1)} %pick_states.1), calls=%async_computation | async-start | bytes 8388608 | tf_op jit(solution)/shard_map/all_to_all | solution.py:491
  16.0 11.0 %copy-start.3 = (f32[3072,4]{0,1:T(4,128)S(1)}, f32[3072,4]{0,1:T(4,128)}, u32[]{:S(2)}) copy-start(f32[3072,4]{0,1:T(4,128)} %param.17) | copy-start | bytes 147460
  16.0 11.0 %copy-start.4 = (f32[3072,4]{0,1:T(4,128)S(1)}, f32[3072,4]{0,1:T(4,128)}, u32[]{:S(2)}) copy-start(f32[3072,4]{0,1:T(4,128)} %param.18) | copy-start | bytes 147460
  16.0 14.3 %copy-start = (bf16[3072,4,128]{2,1,0:T(4,128)(2,1)S(1)}, bf16[3072,4,128]{2,1,0:T(4,128)(2,1)}, u32[]{:S(2)}) copy-start(bf16[3072,4,128]{2,1,0:T(4,128)(2,1)} %param.15) | copy-start | bytes 9437188
  21.3 44.6 %collective-permute-start = (bf16[256,2048]{1,0:T(8,128)(2,1)}, bf16[256,2048]{1,0:T(8,128)(2,1)}, u32[]{:S(2)}, u32[]{:S(2)}) collective-permute-start(bf16[256,2048]{1,0:T(8,128)(2,1)} %constant_dynamic-slice_fusion), channel_id=1, source_target_pairs={{0,1},{1,2},{2,3},{3,0},{4,5},{5,6},{6,7},{7,4},{8,9},{9,10},{10,1... | collective-permute-start | bytes 3145736 | tf_op jit(solution)/shard_map/ppermute | solution.py:511
  22.8 48.8 %collective-permute-start.1 = (bf16[256,2048]{1,0:T(8,128)(2,1)}, bf16[256,2048]{1,0:T(8,128)(2,1)}, u32[]{:S(2)}, u32[]{:S(2)}) collective-permute-start(bf16[256,2048]{1,0:T(8,128)(2,1)} %constant_dynamic-slice_fusion), channel_id=1, source_target_pairs={{0,2},{1,3},{2,0},{3,1},{4,6},{5,7},{6,4},{7,5},{8,10},{9,11},{10,... | collective-permute-start | bytes 3145736 | tf_op jit(solution)/shard_map/ppermute | solution.py:511
  25.5 46.0 %collective-permute-start.2 = (bf16[256,2048]{1,0:T(8,128)(2,1)}, bf16[256,2048]{1,0:T(8,128)(2,1)}, u32[]{:S(2)}, u32[]{:S(2)}) collective-permute-start(bf16[256,2048]{1,0:T(8,128)(2,1)} %constant_dynamic-slice_fusion), channel_id=1, source_target_pairs={{0,3},{1,0},{2,1},{3,2},{4,7},{5,4},{6,5},{7,6},{8,11},{9,8},{10,9... | collective-permute-start | bytes 3145736 | tf_op jit(solution)/shard_map/ppermute | solution.py:511
  30.3 2.2 %copy-start.2 = (bf16[3072,2,128]{2,1,0:T(2,128)(2,1)S(1)}, bf16[3072,2,128]{2,1,0:T(2,128)(2,1)}, u32[]{:S(2)}) copy-start(bf16[3072,2,128]{2,1,0:T(2,128)(2,1)} %param.13) | copy-start | bytes 4718596
  32.5 2.5 %copy-start.1 = (bf16[3072,4,128]{2,1,0:T(4,128)(2,1)S(1)}, bf16[3072,4,128]{2,1,0:T(4,128)(2,1)}, u32[]{:S(2)}) copy-start(bf16[3072,4,128]{2,1,0:T(4,128)(2,1)} %param.16) | copy-start | bytes 9437188
  71.6 7.9 %collective-permute-start.3 = (bf16[256,2048]{1,0:T(8,128)(2,1)}, bf16[256,2048]{1,0:T(8,128)(2,1)}, u32[]{:S(2)}, u32[]{:S(2)}) collective-permute-start(bf16[256,2048]{1,0:T(8,128)(2,1)} %collective-permute-done.refs_2_), channel_id=1, source_target_pairs={{0,4},{4,0},{8,12},{12,8},{16,20},{20,16},{24,28},{28,24},{32,36},... | collective-permute-start | bytes 3145736 | tf_op jit(solution)/shard_map/ppermute | solution.py:528
  71.6 7.9 %collective-permute-start.4 = (bf16[256,2048]{1,0:T(8,128)(2,1)}, bf16[256,2048]{1,0:T(8,128)(2,1)}, u32[]{:S(2)}, u32[]{:S(2)}) collective-permute-start(bf16[256,2048]{1,0:T(8,128)(2,1)} %collective-permute-done.1.refs_2_), channel_id=1, source_target_pairs={{0,4},{4,0},{8,12},{12,8},{16,20},{20,16},{24,28},{28,24},{32,36},... | collective-permute-start | bytes 3145736 | tf_op jit(solution)/shard_map/ppermute | solution.py:528
  72.1 7.4 %collective-permute-start.5 = (bf16[256,2048]{1,0:T(8,128)(2,1)}, bf16[256,2048]{1,0:T(8,128)(2,1)}, u32[]{:S(2)}, u32[]{:S(2)}) collective-permute-start(bf16[256,2048]{1,0:T(8,128)(2,1)} %collective-permute-done.2.refs_3_), channel_id=1, source_target_pairs={{0,4},{4,0},{8,12},{12,8},{16,20},{20,16},{24,28},{28,24},{32,36},... | collective-permute-start | bytes 3145736 | tf_op jit(solution)/shard_map/ppermute | solution.py:528
  79.4 60.9 %all-to-all-start.1 = ((bf16[32,4,128,128]{3,2,1,0:T(8,128)(2,1)}), bf16[32,4,128,128]{3,2,1,0:T(8,128)(2,1)}, u32[]{:S(2)}, u32[]{:S(2)}) async-start(bf16[32,4,128,128]{3,2,1,0:T(8,128)(2,1)} %finish.1), calls=%async_computation.1 | async-start | bytes 8388608 | tf_op jit(solution)/shard_map/all_to_all | solution.py:531
  91.7 14.5 %copy-start.5 = (s32[768]{0:T(1024)S(1)}, s32[768]{0:T(1024)}, u32[]{:S(2)}) copy-start(s32[768]{0:T(1024)} %param.25) | copy-start | bytes 9220
  91.7 22.3 %collective-permute-start.8 = (bf16[768,512]{1,0:T(8,128)(2,1)}, bf16[768,512]{1,0:T(8,128)(2,1)}, u32[]{:S(2)}, u32[]{:S(2)}) collective-permute-start(bf16[768,512]{1,0:T(8,128)(2,1)} %emit.3), channel_id=1, source_target_pairs={{0,2},{1,3},{2,0},{3,1},{4,6},{5,7},{6,4},{7,5},{8,10},{9,11},{10,... | collective-permute-start | bytes 2359304 | tf_op jit(solution)/shard_map/ppermute | solution.py:541
  102.9 26.9 %collective-permute-start.6 = (bf16[768,512]{1,0:T(8,128)(2,1)}, bf16[768,512]{1,0:T(8,128)(2,1)}, u32[]{:S(2)}, u32[]{:S(2)}) collective-permute-start(bf16[768,512]{1,0:T(8,128)(2,1)} %get-tuple-element.34), channel_id=1, source_target_pairs={{0,1},{1,2},{2,3},{3,0},{4,5},{5,6},{6,7},{7,4},{8,9},{9,10},{10,1... | collective-permute-start | bytes 2359304 | tf_op jit(solution)/shard_map/ppermute | solution.py:541
  103.3 26.5 %collective-permute-start.7 = (bf16[768,512]{1,0:T(8,128)(2,1)}, bf16[768,512]{1,0:T(8,128)(2,1)}, u32[]{:S(2)}, u32[]{:S(2)}) collective-permute-start(bf16[768,512]{1,0:T(8,128)(2,1)} %get-tuple-element.35), channel_id=1, source_target_pairs={{0,3},{1,0},{2,1},{3,2},{4,7},{5,4},{6,5},{7,6},{8,11},{9,8},{10,9... | collective-permute-start | bytes 2359304 | tf_op jit(solution)/shard_map/ppermute | solution.py:541

commit v3 on v2

--- a/solution.py
+++ b/solution.py
@@ -29,18 +29,29 @@
     return pltpu.CompilerParams(vmem_limit_bytes=(64 << 20) - (1 << 18))
 
 
-def pick_kernel(wanted_ref, cache_ref, out_ref, wide, short, in_sems, out_sems):
+def pick_kernel(device_ref, owner_ref, slot_ref, cache_ref, out_ref, wide, short, wanted, in_sems, out_sems):
     slots, count = cache_ref.shape[0], out_ref.shape[0]
+    requests = owner_ref.shape[0] // count
     loads = [
         pltpu.make_async_copy(cache_ref.at[i], wide.at[i], in_sems.at[i]) for i in range(slots)
     ]
     for load in loads:
         load.start()
+    device = device_ref[0]
+
+    @pl.loop(0, count)
+    def _(i):
+        slot = 0
+        for j in range(requests):
+            at = i * requests + j
+            slot = jnp.where(owner_ref[at] == device, slot_ref[at], slot)
+        wanted[i] = slot
+
     for i, load in enumerate(loads):
         load.wait()
         short[i] = wide[i].astype(BF16)
     stores = [
-        pltpu.make_async_copy(short.at[wanted_ref[i]], out_ref.at[i], out_sems.at[i])
+        pltpu.make_async_copy(short.at[wanted[i]], out_ref.at[i], out_sems.at[i])
         for i in range(count)
     ]
     for store in stores:
@@ -49,20 +60,20 @@
         store.wait()
 
 
-def pick_states(wanted, cache_states):
-    count = wanted.shape[0]
+def pick_states(device, count, owners, slots, cache_states):
     one = cache_states.shape[1:]
     return pl.pallas_call(
         pick_kernel,
         out_shape=jax.ShapeDtypeStruct((count,) + one, BF16),
         grid_spec=pltpu.PrefetchScalarGridSpec(
-            num_scalar_prefetch=1,
+            num_scalar_prefetch=3,
             grid=(1,),
             in_specs=[pl.BlockSpec(memory_space=pl.ANY)],
             out_specs=pl.BlockSpec(memory_space=pl.ANY),
             scratch_shapes=[
                 pltpu.VMEM(cache_states.shape, F32),
                 pltpu.VMEM(cache_states.shape, BF16),
+                pltpu.SMEM((count,), jnp.int32),
                 pltpu.SemaphoreType.DMA((cache_states.shape[0],)),
                 pltpu.SemaphoreType.DMA((count,)),
             ],
@@ -70,7 +81,7 @@
         compiler_params=params(),
         cost_estimate=pl.CostEstimate(flops=0, bytes_accessed=6 << 20, transcendentals=0),
         name="pick_states",
-    )(wanted, cache_states)
+    )(device, owners, slots, cache_states)
 
 
 def unit_rows(vectors):
@@ -485,13 +496,12 @@
     chunks = queries.shape[1]
     heads = heads_all // chunks
 
-    naming = cache_owner.reshape(owner_count, requests) == device
-    wanted = jnp.sum(jnp.where(naming, cache_slot.reshape(owner_count, requests), 0), axis=1)
-    picked = pick_states(wanted, cache_states)
+    picked = pick_states(device.reshape(1), owner_count, cache_owner, cache_slot, cache_states)
     arrived = lax.all_to_all(picked, "req", split_axis=0, concat_axis=0, tiled=True)
 
     my_owner = lax.dynamic_slice_in_dim(cache_owner, device * requests, requests)
     my_blocks = lax.dynamic_slice_in_dim(suffix_blocks, device * requests, requests)
+    naming = cache_owner.reshape(owner_count, requests) == device
     slot_ids = jnp.arange(requests, dtype=jnp.int32)
     claimed = naming[None] & (
         new_slot.reshape(owner_count, requests)[None] == slot_ids[:, None, None]
@@ -505,7 +515,7 @@
     gate_flat = gate_input.reshape(tokens, -1)
     half = out_weight.shape[0] // 2
     core = device % 2
-    out_weight, key_flat = lax.optimization_barrier((out_weight, key_flat))
+    out_weight, my_owner = lax.optimization_barrier((out_weight, my_owner))
     own_rows = lax.dynamic_slice_in_dim(out_weight, core * half, half)
     nears = [
         lax.ppermute(own_rows, "head", [(i, (i + d) % groups) for i in range(groups)])

time: 146 us -> 142 us (0.973)
  local copies, waits for them, and re-layouts: 15.9 us -> 11.8 us
    unnamed x16 -> x18, local copies, waits for them, and re-layouts: 9.79 us -> 5.07 us
  transfers between devices with their start and end apart: 11 -> 11, of which waited for: 4 -> 5; matrix products, arithmetic and copies ran while one was open for 11% -> 9% of each run, Pallas kernels for 44% -> 46%
where the time goes in v3:
time: 142 us; the launch traced here: 141 us
  Pallas kernels  73.6 us (52%)
  starting transfers between devices  28.3 us (20%)
  waiting for transfers between devices  24.5 us (17%)
  local copies, waits for them, and re-layouts  11.8 us (8%)
  other arithmetic  1.83 us (1%)
    pallas_call x1, Pallas kernels, prepare(): pl.pallas_call(functools.partial(prep_kernel, per_step), out_shape=(jax.S...  28.7 us
    pallas_call x2, Pallas kernels, project(): pl.pallas_call(functools.partial(project_kernel, len(shares), half), out_...  15.2 us
    ppermute x3, waiting for transfers between devices, local(): shares[d] = lax.ppermute(share, 'head', pairs) if d else share  15 us
    pallas_call x2, Pallas kernels, emit(): pl.pallas_call(functools.partial(emit_kernel, per_step, group_steps, grou...  13.1 us
    all_to_all x1, starting transfers between devices, local(): lax.all_to_all(picked, 'req', split_axis=0, concat_axis=0, tiled=True)  8.69 us
    all_to_all x1, starting transfers between devices, local(): lax.all_to_all(final, 'req', split_axis=0, concat_axis=0, tiled=True)  7.51 us
    pallas_call x1, Pallas kernels, finish(): pl.pallas_call(finish_kernel, out_shape=jax.ShapeDtypeStruct(states.shape...  7.24 us
    ppermute x3, waiting for transfers between devices, local(): lax.ppermute(own_rows, 'head', [(i, (i + d) % groups) for i in range(grou...  6.66 us
  transfers between devices with their start and end apart: 11, of which 5 were waited for; matrix products, arithmetic and copies ran while one was open for 9% of the time, Pallas kernels for 46%

profile of v3, /device:TPU:0, one launch (start us, length us, event | category | flops | bytes accessed | tf_op | source)
XLA Modules:
  0.0 140.9 jit_solution(10339402188194689594)
XLA Ops:
  0.6 4.7 %pick_states.1 = bf16[32,4,128,128]{3,2,1,0:T(8,128)(2,1)} custom-call(s32[1]{0:T(128)} %bitcast.device_ref, s32[768]{0:T(1024)} %owner_ref.1, s32[768]{0:T(1024)} %slot_ref.1, f32[8,4,128,128]{3,2,1,0:T(8,128)} %cache_ref.1), custom_call_target="tpu_custom_call" | custom-call | bytes 6291456 | tf_op jit(solution)/shard_map/pick_states/pallas_call | solution.py:65
  5.4 8.7 %all-to-all-start = ((bf16[32,4,128,128]{3,2,1,0:T(8,128)(2,1)}), bf16[32,4,128,128]{3,2,1,0:T(8,128)(2,1)}, u32[]{:S(2)}, u32[]{:S(2)}) async-start(bf16[32,4,128,128]{3,2,1,0:T(8,128)(2,1)} %pick_states.1), calls=%async_computation | async-start | bytes 8388608 | tf_op jit(solution)/shard_map/all_to_all | solution.py:500
  14.1 0.6 dynamic_slice.9.owner_ref
  14.7 2.4 %constant_dynamic-slice_fusion = bf16[256,2048]{1,0:T(8,128)(2,1)} fusion(bf16[512,2048]{1,0:T(8,128)(2,1)} %refs_5_, s32[]{:T(128)S(6)} %select_n.20), kind=kLoop, calls=%fused_computation.9 | loop fusion | bytes 2097156 | tf_op jit(solution)/shard_map/dynamic_slice | solution.py:519
  17.1 1.5 %collective-permute-start = (bf16[256,2048]{1,0:T(8,128)(2,1)}, bf16[256,2048]{1,0:T(8,128)(2,1)}, u32[]{:S(2)}, u32[]{:S(2)}) collective-permute-start(bf16[256,2048]{1,0:T(8,128)(2,1)} %constant_dynamic-slice_fusion), channel_id=1, source_target_pairs={{0,1},{1,2},{2,3},{3,0},{4,5},{5,6},{6,7},{7,4},{8,9},{9,10},{10,1... | collective-permute-start | bytes 3145736 | tf_op jit(solution)/shard_map/ppermute | solution.py:521
  18.6 2.7 %collective-permute-start.1 = (bf16[256,2048]{1,0:T(8,128)(2,1)}, bf16[256,2048]{1,0:T(8,128)(2,1)}, u32[]{:S(2)}, u32[]{:S(2)}) collective-permute-start(bf16[256,2048]{1,0:T(8,128)(2,1)} %constant_dynamic-slice_fusion), channel_id=1, source_target_pairs={{0,2},{1,3},{2,0},{3,1},{4,6},{5,7},{6,4},{7,5},{8,10},{9,11},{10,... | collective-permute-start | bytes 3145736 | tf_op jit(solution)/shard_map/ppermute | solution.py:521
  21.3 1.4 %collective-permute-start.2 = (bf16[256,2048]{1,0:T(8,128)(2,1)}, bf16[256,2048]{1,0:T(8,128)(2,1)}, u32[]{:S(2)}, u32[]{:S(2)}) collective-permute-start(bf16[256,2048]{1,0:T(8,128)(2,1)} %constant_dynamic-slice_fusion), channel_id=1, source_target_pairs={{0,3},{1,0},{2,1},{3,2},{4,7},{5,4},{6,5},{7,6},{8,11},{9,8},{10,9... | collective-permute-start | bytes 3145736 | tf_op jit(solution)/shard_map/ppermute | solution.py:521
  22.9 2.1 %copy_bitcast_fusion.2 = (bf16[3072,256]{1,0:T(8,128)(2,1)}, bf16[3072,256]{1,0:T(8,128)(2,1)}) fusion(bf16[384,8,2,128]{3,2,1,0:T(2,128)(2,1)S(1)} %bitcast.25, bf16[384,8,2,128]{3,2,1,0:T(2,128)(2,1)S(1)} %bitcast.26), kind=kLoop, calls=%fused_computation.2 | loop fusion | bytes 6291456 | tf_op jit(solution)/shard_map/reshape | solution.py:513
  25.0 0.7 pad_maximum_fusion.rows_ref
  25.7 1.2 dynamic_slice.11.blocks_ref
  26.9 2.2 %copy.25 = bf16[384,8,4,128]{3,1,2,0:T(8,128)(2,1)} copy(bf16[384,8,4,128]{3,2,1,0:T(4,128)(2,1)S(1)} %bitcast.22) | data formatting | bytes 6291456
  29.1 0.7 copy-done.1
  29.8 2.2 %copy.26 = bf16[384,8,4,128]{3,1,2,0:T(8,128)(2,1)} copy(bf16[384,8,4,128]{3,2,1,0:T(4,128)(2,1)S(1)} %bitcast.23) | data formatting | bytes 6291456
  32.0 28.7 %prepare.1 = (bf16[24,4,256,128]{3,2,1,0:T(8,128)(2,1)}, bf16[24,4,256,128]{3,2,1,0:T(8,128)(2,1)}) custom-call(s32[24]{0:T(128)} %dynamic_slice.11.blocks_ref, bf16[3072,256]{1,0:T(8,128)(2,1)} %get-tuple-element.43.q_ref, bf16[3072,256]{1,0:T(8,128)(2,1)} %get-tuple-element.42.k_ref, bf16[3072,512]{1,0:T(8,128)(2,1)} %bitcast.24, ...), custom_call_target="tpu_custom_call" | custom-call | flops 9663676416 | bytes 25165824 | tf_op jit(solution)/shard_map/prepare/pallas_call | solution.py:229
  60.7 6.7 %collective-permute-done.1.refs_2_ = bf16[256,2048]{1,0:T(8,128)(2,1)} collective-permute-done((bf16[256,2048]{1,0:T(8,128)(2,1)}, bf16[256,2048]{1,0:T(8,128)(2,1)}, u32[]{:S(2)}, u32[]{:S(2)}) %collective-permute-start.1) | collective-permute-done | bytes 1048608 | tf_op jit(solution)/shard_map/ppermute | solution.py:521
  67.3 0.2 all-to-all-done.state_ref.refs_0_.refs_1_.refs_2_.refs_3_.refs_4_.refs_5_
  67.5 0.5 collective-permute-start.4
  68.1 7.2 %finish.1 = bf16[32,4,128,128]{3,2,1,0:T(8,128)(2,1)} custom-call(s32[24]{0:T(128)} %dynamic_slice.9.owner_ref, bf16[32,4,128,128]{3,2,1,0:T(8,128)(2,1)} %all-to-all-done.state_ref.refs_0_.refs_1_.refs_2_.refs_3_.refs_4_.refs_5_, bf16[24,4,256,128]{3,2,1,0:T(8,128)(2,1)} %get-tuple-element.30.maps_ref), custom_call_target="tpu_custom_call" | custom-call | flops 402653184 | bytes 13631488 | tf_op jit(solution)/shard_map/finish/pallas_call | solution.py:279
  75.3 7.5 %all-to-all-start.1 = ((bf16[32,4,128,128]{3,2,1,0:T(8,128)(2,1)}), bf16[32,4,128,128]{3,2,1,0:T(8,128)(2,1)}, u32[]{:S(2)}, u32[]{:S(2)}) async-start(bf16[32,4,128,128]{3,2,1,0:T(8,128)(2,1)} %finish.1), calls=%async_computation.1 | async-start | bytes 8388608 | tf_op jit(solution)/shard_map/all_to_all | solution.py:541
  82.9 4.6 %emit.3 = bf16[768,512]{1,0:T(8,128)(2,1)} custom-call(s32[24]{0:T(128)} %dynamic_slice.9.owner_ref, s32[24]{0:T(128)} %dynamic_slice.11.blocks_ref, s32[1]{0:T(128)} %bitcast.4.group_ref, bf16[32,4,128,128]{3,2,1,0:T(8,128)(2,1)} %all-to-all-done.state_ref.refs_0_.refs_1_.refs_2_.refs_3_.refs_4_.refs_5_, ...), custom_call_target="tpu_custom_call" | custom-call | flops 402653184 | bytes 16777216 | tf_op jit(solution)/shard_map/emit/pallas_call | solution.py:361
  87.4 2.7 %collective-permute-start.8 = (bf16[768,512]{1,0:T(8,128)(2,1)}, bf16[768,512]{1,0:T(8,128)(2,1)}, u32[]{:S(2)}, u32[]{:S(2)}) collective-permute-start(bf16[768,512]{1,0:T(8,128)(2,1)} %emit.3), channel_id=1, source_target_pairs={{0,2},{1,3},{2,0},{3,1},{4,6},{5,7},{6,4},{7,5},{8,10},{9,11},{10,... | collective-permute-start | bytes 2359304 | tf_op jit(solution)/shard_map/ppermute | solution.py:551
  90.1 8.6 %emit.2 = (bf16[768,512]{1,0:T(8,128)(2,1)}, bf16[768,512]{1,0:T(8,128)(2,1)}, bf16[768,512]{1,0:T(8,128)(2,1)}) custom-call(s32[24]{0:T(128)} %dynamic_slice.9.owner_ref, s32[24]{0:T(128)} %dynamic_slice.11.blocks_ref, s32[1]{0:T(128)} %bitcast.4.group_ref, bf16[32,4,128,128]{3,2,1,0:T(8,128)(2,1)} %all-to-all-done.state_ref.refs_0_.refs_1_.refs_2_.refs_3_.refs_4_.refs_5_, ...), custom_call_target="tpu_custom_call" | custom-call | flops 402653184 | bytes 16777216 | tf_op jit(solution)/shard_map/emit/pallas_call | solution.py:361
  98.7 0.5 collective-permute-start.6
  99.1 2.8 %collective-permute-start.7 = (bf16[768,512]{1,0:T(8,128)(2,1)}, bf16[768,512]{1,0:T(8,128)(2,1)}, u32[]{:S(2)}, u32[]{:S(2)}) collective-permute-start(bf16[768,512]{1,0:T(8,128)(2,1)} %get-tuple-element.35), channel_id=1, source_target_pairs={{0,3},{1,0},{2,1},{3,2},{4,7},{5,4},{6,5},{7,6},{8,11},{9,8},{10,9... | collective-permute-start | bytes 2359304 | tf_op jit(solution)/shard_map/ppermute | solution.py:551
  101.9 0.1 eq.32
  102.3 1.1 select_reduce_fusion.source_ref
  103.4 6.3 %collective-permute-done.8.refs_0_ = bf16[768,512]{1,0:T(8,128)(2,1)} collective-permute-done((bf16[768,512]{1,0:T(8,128)(2,1)}, bf16[768,512]{1,0:T(8,128)(2,1)}, u32[]{:S(2)}, u32[]{:S(2)}) %collective-permute-start.8) | collective-permute-done | bytes 786464 | tf_op jit(solution)/shard_map/ppermute | solution.py:551
  109.7 7.2 %project.2.refs_6_ = bf16[768,2048]{1,0:T(8,128)(2,1)} custom-call(s32[1]{0:T(128)} %bitcast.3.place_ref, bf16[768,512]{1,0:T(8,128)(2,1)} %collective-permute-done.8.refs_0_, bf16[768,512]{1,0:T(8,128)(2,1)} %get-tuple-element.38.refs_1_, bf16[256,2048]{1,0:T(8,128)(2,1)} %collective-permute-done.1.refs_2_, bf16[512,2048]{1,0:T(8,128)(2,1)} %refs_5_, ...), custom_call_target="tpu_custom_call" | custom-call | flops 3221225472 | bytes 12582912 | tf_op jit(solution)/shard_map/project/pallas_call | solution.py:455
  116.9 8.7 %collective-permute-done.6.refs_0_ = bf16[768,512]{1,0:T(8,128)(2,1)} collective-permute-done((bf16[768,512]{1,0:T(8,128)(2,1)}, bf16[768,512]{1,0:T(8,128)(2,1)}, u32[]{:S(2)}, u32[]{:S(2)}) %collective-permute-start.6) | collective-permute-done | bytes 786464 | tf_op jit(solution)/shard_map/ppermute | solution.py:551
  125.6 7.9 %project.3 = bf16[768,2048]{1,0:T(8,128)(2,1)} custom-call(s32[1]{0:T(128)} %bitcast.3.place_ref, bf16[768,512]{1,0:T(8,128)(2,1)} %collective-permute-done.6.refs_0_, bf16[768,512]{1,0:T(8,128)(2,1)} %collective-permute-done.7.refs_1_, bf16[256,2048]{1,0:T(8,128)(2,1)} %collective-permute-done.refs_2_, bf16[256,2048]{1,0:T(8,128)(2,1)} %collective-permute-done.2.refs_3_, ...), custom_call_target="tpu_custom_call" | custom-call | flops 3221225472 | bytes 12582912 | tf_op jit(solution)/shard_map/project/pallas_call | solution.py:455
  133.5 2.6 %all-to-all-done.1.arrived_ref = bf16[32,4,128,128]{3,2,1,0:T(8,128)(2,1)} async-done(((bf16[32,4,128,128]{3,2,1,0:T(8,128)(2,1)}), bf16[32,4,128,128]{3,2,1,0:T(8,128)(2,1)}, u32[]{:S(2)}, u32[]{:S(2)}) %all-to-all-start.1) | async-done | bytes 4194336 | tf_op jit(solution)/shard_map/all_to_all | solution.py:541
  136.2 4.6 %place.1 = f32[24,4,128,128]{3,2,1,0:T(8,128)} custom-call(s32[24]{0:T(128)} %select_reduce_fusion.source_ref, bf16[32,4,128,128]{3,2,1,0:T(8,128)(2,1)} %all-to-all-done.1.arrived_ref), custom_call_target="tpu_custom_call" | custom-call | bytes 10485760 | tf_op jit(solution)/shard_map/place/pallas_call | solution.py:408
  (29 shorter events, 0.4 us)
Async XLA Ops:
  5.3 8.8 %copy-start.6 = (s32[768]{0:T(1024)S(1)}, s32[768]{0:T(1024)}, u32[]{:S(2)}) copy-start(s32[768]{0:T(1024)} %owner_ref.1) | copy-start | bytes 9220
  5.3 17.4 %copy-start.4 = (f32[3072,4]{0,1:T(4,128)S(1)}, f32[3072,4]{0,1:T(4,128)}, u32[]{:S(2)}) copy-start(f32[3072,4]{0,1:T(4,128)} %param.17) | copy-start | bytes 147460
  5.4 17.4 %copy-start.5 = (f32[3072,4]{0,1:T(4,128)S(1)}, f32[3072,4]{0,1:T(4,128)}, u32[]{:S(2)}) copy-start(f32[3072,4]{0,1:T(4,128)} %param.18) | copy-start | bytes 147460
  5.4 17.5 %copy-start.3 = (bf16[3072,2,128]{2,1,0:T(2,128)(2,1)S(1)}, bf16[3072,2,128]{2,1,0:T(2,128)(2,1)}, u32[]{:S(2)}) copy-start(bf16[3072,2,128]{2,1,0:T(2,128)(2,1)} %param.13) | copy-start | bytes 4718596
  5.4 62.2 %all-to-all-start = ((bf16[32,4,128,128]{3,2,1,0:T(8,128)(2,1)}), bf16[32,4,128,128]{3,2,1,0:T(8,128)(2,1)}, u32[]{:S(2)}, u32[]{:S(2)}) async-start(bf16[32,4,128,128]{3,2,1,0:T(8,128)(2,1)} %pick_states.1), calls=%async_computation | async-start | bytes 8388608 | tf_op jit(solution)/shard_map/all_to_all | solution.py:500
  14.1 8.8 %copy-start.2 = (bf16[3072,2,128]{2,1,0:T(2,128)(2,1)S(1)}, bf16[3072,2,128]{2,1,0:T(2,128)(2,1)}, u32[]{:S(2)}) copy-start(bf16[3072,2,128]{2,1,0:T(2,128)(2,1)} %param.14) | copy-start | bytes 4718596
  17.1 43.6 %collective-permute-start = (bf16[256,2048]{1,0:T(8,128)(2,1)}, bf16[256,2048]{1,0:T(8,128)(2,1)}, u32[]{:S(2)}, u32[]{:S(2)}) collective-permute-start(bf16[256,2048]{1,0:T(8,128)(2,1)} %constant_dynamic-slice_fusion), channel_id=1, source_target_pairs={{0,1},{1,2},{2,3},{3,0},{4,5},{5,6},{6,7},{7,4},{8,9},{9,10},{10,1... | collective-permute-start | bytes 3145736 | tf_op jit(solution)/shard_map/ppermute | solution.py:521
  18.6 48.8 %collective-permute-start.1 = (bf16[256,2048]{1,0:T(8,128)(2,1)}, bf16[256,2048]{1,0:T(8,128)(2,1)}, u32[]{:S(2)}, u32[]{:S(2)}) collective-permute-start(bf16[256,2048]{1,0:T(8,128)(2,1)} %constant_dynamic-slice_fusion), channel_id=1, source_target_pairs={{0,2},{1,3},{2,0},{3,1},{4,6},{5,7},{6,4},{7,5},{8,10},{9,11},{10,... | collective-permute-start | bytes 3145736 | tf_op jit(solution)/shard_map/ppermute | solution.py:521
  21.3 46.0 %collective-permute-start.2 = (bf16[256,2048]{1,0:T(8,128)(2,1)}, bf16[256,2048]{1,0:T(8,128)(2,1)}, u32[]{:S(2)}, u32[]{:S(2)}) collective-permute-start(bf16[256,2048]{1,0:T(8,128)(2,1)} %constant_dynamic-slice_fusion), channel_id=1, source_target_pairs={{0,3},{1,0},{2,1},{3,2},{4,7},{5,4},{6,5},{7,6},{8,11},{9,8},{10,9... | collective-permute-start | bytes 3145736 | tf_op jit(solution)/shard_map/ppermute | solution.py:521
  22.9 4.1 %copy-start = (bf16[3072,4,128]{2,1,0:T(4,128)(2,1)S(1)}, bf16[3072,4,128]{2,1,0:T(4,128)(2,1)}, u32[]{:S(2)}) copy-start(bf16[3072,4,128]{2,1,0:T(4,128)(2,1)} %param.15) | copy-start | bytes 9437188
  26.9 2.9 %copy-start.1 = (bf16[3072,4,128]{2,1,0:T(4,128)(2,1)S(1)}, bf16[3072,4,128]{2,1,0:T(4,128)(2,1)}, u32[]{:S(2)}) copy-start(bf16[3072,4,128]{2,1,0:T(4,128)(2,1)} %param.16) | copy-start | bytes 9437188
  67.5 7.8 %collective-permute-start.3 = (bf16[256,2048]{1,0:T(8,128)(2,1)}, bf16[256,2048]{1,0:T(8,128)(2,1)}, u32[]{:S(2)}, u32[]{:S(2)}) collective-permute-start(bf16[256,2048]{1,0:T(8,128)(2,1)} %collective-permute-done.refs_2_), channel_id=1, source_target_pairs={{0,4},{4,0},{8,12},{12,8},{16,20},{20,16},{24,28},{28,24},{32,36},... | collective-permute-start | bytes 3145736 | tf_op jit(solution)/shard_map/ppermute | solution.py:538
  67.5 7.8 %collective-permute-start.4 = (bf16[256,2048]{1,0:T(8,128)(2,1)}, bf16[256,2048]{1,0:T(8,128)(2,1)}, u32[]{:S(2)}, u32[]{:S(2)}) collective-permute-start(bf16[256,2048]{1,0:T(8,128)(2,1)} %collective-permute-done.1.refs_2_), channel_id=1, source_target_pairs={{0,4},{4,0},{8,12},{12,8},{16,20},{20,16},{24,28},{28,24},{32,36},... | collective-permute-start | bytes 3145736 | tf_op jit(solution)/shard_map/ppermute | solution.py:538
  68.1 7.3 %collective-permute-start.5 = (bf16[256,2048]{1,0:T(8,128)(2,1)}, bf16[256,2048]{1,0:T(8,128)(2,1)}, u32[]{:S(2)}, u32[]{:S(2)}) collective-permute-start(bf16[256,2048]{1,0:T(8,128)(2,1)} %collective-permute-done.2.refs_3_), channel_id=1, source_target_pairs={{0,4},{4,0},{8,12},{12,8},{16,20},{20,16},{24,28},{28,24},{32,36},... | collective-permute-start | bytes 3145736 | tf_op jit(solution)/shard_map/ppermute | solution.py:538
  75.3 60.8 %all-to-all-start.1 = ((bf16[32,4,128,128]{3,2,1,0:T(8,128)(2,1)}), bf16[32,4,128,128]{3,2,1,0:T(8,128)(2,1)}, u32[]{:S(2)}, u32[]{:S(2)}) async-start(bf16[32,4,128,128]{3,2,1,0:T(8,128)(2,1)} %finish.1), calls=%async_computation.1 | async-start | bytes 8388608 | tf_op jit(solution)/shard_map/all_to_all | solution.py:541
  87.4 14.7 %copy-start.7 = (s32[768]{0:T(1024)S(1)}, s32[768]{0:T(1024)}, u32[]{:S(2)}) copy-start(s32[768]{0:T(1024)} %param.25) | copy-start | bytes 9220
  87.4 22.3 %collective-permute-start.8 = (bf16[768,512]{1,0:T(8,128)(2,1)}, bf16[768,512]{1,0:T(8,128)(2,1)}, u32[]{:S(2)}, u32[]{:S(2)}) collective-permute-start(bf16[768,512]{1,0:T(8,128)(2,1)} %emit.3), channel_id=1, source_target_pairs={{0,2},{1,3},{2,0},{3,1},{4,6},{5,7},{6,4},{7,5},{8,10},{9,11},{10,... | collective-permute-start | bytes 2359304 | tf_op jit(solution)/shard_map/ppermute | solution.py:551
  98.7 26.9 %collective-permute-start.6 = (bf16[768,512]{1,0:T(8,128)(2,1)}, bf16[768,512]{1,0:T(8,128)(2,1)}, u32[]{:S(2)}, u32[]{:S(2)}) collective-permute-start(bf16[768,512]{1,0:T(8,128)(2,1)} %get-tuple-element.34), channel_id=1, source_target_pairs={{0,1},{1,2},{2,3},{3,0},{4,5},{5,6},{6,7},{7,4},{8,9},{9,10},{10,1... | collective-permute-start | bytes 2359304 | tf_op jit(solution)/shard_map/ppermute | solution.py:551
  99.1 26.5 %collective-permute-start.7 = (bf16[768,512]{1,0:T(8,128)(2,1)}, bf16[768,512]{1,0:T(8,128)(2,1)}, u32[]{:S(2)}, u32[]{:S(2)}) collective-permute-start(bf16[768,512]{1,0:T(8,128)(2,1)} %get-tuple-element.35), channel_id=1, source_target_pairs={{0,3},{1,0},{2,1},{3,2},{4,7},{5,4},{6,5},{7,6},{8,11},{9,8},{10,9... | collective-permute-start | bytes 2359304 | tf_op jit(solution)/shard_map/ppermute | solution.py:551
